TPU v7x, 32 devices: a whole 2x2x4 slice. The times are simulated.
32 devices in a mesh: grp: 4 (over y, x), shard: 8 (over z, core).
Axes of the slice: x: 2, y: 2, z: 4, core: 2. Of those that a mesh axis runs over, the one named last changes fastest.
Arguments:
- moe_input: bfloat16 [4096, 2048], P(('grp', 'shard')), may hold values from -6 to 6
- out_grad: bfloat16 [4096, 2048], P(('grp', 'shard')), may hold values from -6 to 6
- expert_ids: int32 [4096, 2], P(('grp', 'shard')), may hold values from 0 to 127, all different within a row; in each aligned block of 128 rows (0 to 127, 128 to 255, ...) at most 3 rows name the same one
- gate_weights: bfloat16 [4096, 2], P(('grp', 'shard')), may hold values from 0.099609375 to 1
- w_gate: bfloat16 [128, 768, 2048], P('shard', 'grp'), may hold values from -0.125 to 0.125
- w_up: bfloat16 [128, 768, 2048], P('shard', 'grp'), may hold values from -0.125 to 0.125
- w_down: bfloat16 [128, 768, 2048], P('shard', 'grp'), may hold values from -0.21875 to 0.21875
Outputs:
- input_grad: bfloat16 [4096, 2048], P(('grp', 'shard'))
- grad_gate: bfloat16 [128, 768, 2048], P('shard', 'grp')
- grad_up: bfloat16 [128, 768, 2048], P('shard', 'grp')
- grad_down: bfloat16 [128, 768, 2048], P('shard', 'grp')
Inputs may be any that keep to these rules, and one draw needn't show every extreme that they name: `expert_ids`: each token names 2 different experts; within the 128 tokens of one device no expert is named more than 3 times, a bound that some block reaches.
All inputs are finite; a program needn't handle non-finite values.
Results may differ from a plain program's by a relative error of at most 0.0058.
Values may be sent and summed in bfloat16 or wider, within the bound.
A program may use at most 192 MiB of HBM per device.

v0:
```python
import jax
import jax.numpy as jnp
from jax import lax
from jax.sharding import PartitionSpec as P

EXPERTS = 128
TOP = 2
CAP = 3


def silu_parts(pre_act):
    sigmoid_val = jax.nn.sigmoid(pre_act)
    return (pre_act * sigmoid_val, sigmoid_val * (1.0 + pre_act * (1.0 - sigmoid_val)))


def slot_maps(ids_here, per_device, shards):
    tokens_here = ids_here.shape[0]
    flat_ids = ids_here.reshape(tokens_here * TOP)
    matches = (flat_ids[:, None] == jnp.arange(EXPERTS, dtype=jnp.int32)[None, :]).astype(jnp.int32)
    rank_of = jnp.sum((jnp.cumsum(matches, axis=0) - matches) * matches, axis=1)
    slot_of = flat_ids % per_device * (shards * CAP) + flat_ids // per_device * CAP + rank_of
    return (slot_of[:, None] == jnp.arange(EXPERTS * CAP, dtype=jnp.int32)[None, :]).astype(
        jnp.float32
    )


def body(moe_input, out_grad, expert_ids, gate_weights, w_gate, w_up, w_down):
    contract_rows = (((0,), (0,)), ((), ()))
    shards = lax.axis_size("shard")
    groups = lax.axis_size("grp")
    per_device = w_gate.shape[0]
    tokens_here = moe_input.shape[0]
    model_width = moe_input.shape[1]
    chosen = slot_maps(expert_ids, per_device, shards)
    slot_total = EXPERTS * CAP
    token_map = jnp.sum(chosen.reshape(tokens_here, TOP, slot_total), axis=1)
    gate_slots = jnp.dot(
        gate_weights.reshape(tokens_here * TOP).astype(jnp.float32),
        chosen,
        precision=lax.Precision.HIGHEST,
    ).astype(jnp.bfloat16)
    map_low = token_map.astype(jnp.bfloat16)
    input_slots = lax.dot_general(
        map_low, moe_input, contract_rows, preferred_element_type=jnp.float32
    ).astype(jnp.bfloat16)
    grad_slots = lax.dot_general(
        map_low, out_grad, contract_rows, preferred_element_type=jnp.float32
    ).astype(jnp.bfloat16)
    slot_shape = (per_device, shards, CAP, model_width)
    arrived = (
        lax.all_to_all(
            input_slots.reshape(slot_shape), "shard", split_axis=1, concat_axis=1, tiled=True
        ),
        lax.all_to_all(
            grad_slots.reshape(slot_shape), "shard", split_axis=1, concat_axis=1, tiled=True
        ),
        lax.all_to_all(
            gate_slots.reshape(per_device, shards, CAP),
            "shard",
            split_axis=1,
            concat_axis=1,
            tiled=True,
        ),
    )
    inputs, grads_in, gate_rows = (
        lax.all_gather(arrived[0], "grp", axis=1, tiled=True),
        lax.all_gather(arrived[1], "grp", axis=1, tiled=True),
        lax.all_gather(arrived[2], "grp", axis=1, tiled=True),
    )
    row_count = groups * shards * CAP
    inputs = inputs.reshape(per_device, row_count, model_width)
    grads_in = grads_in.reshape(per_device, row_count, model_width)
    gate_rows = gate_rows.reshape(per_device, row_count)
    gated = (gate_rows.astype(jnp.float32)[:, :, None] * grads_in.astype(jnp.float32)).astype(
        jnp.bfloat16
    )
    pre_gate = jnp.einsum("efd,erd->efr", w_gate, inputs, preferred_element_type=jnp.float32)
    pre_up = jnp.einsum("efd,erd->efr", w_up, inputs, preferred_element_type=jnp.float32)
    act_val, act_slope = silu_parts(pre_gate)
    activation = (act_val * pre_up).astype(jnp.bfloat16)
    act_grad = jnp.einsum("efd,erd->efr", w_down, gated, preferred_element_type=jnp.float32)
    gate_grad = (act_grad * pre_up * act_slope).astype(jnp.bfloat16)
    up_grad = (act_grad * act_val).astype(jnp.bfloat16)
    grad_down = jnp.einsum(
        "efr,erd->efd", activation, gated, preferred_element_type=jnp.float32
    ).astype(jnp.bfloat16)
    grad_gate = jnp.einsum(
        "efr,erd->efd", gate_grad, inputs, preferred_element_type=jnp.float32
    ).astype(jnp.bfloat16)
    grad_up = jnp.einsum(
        "efr,erd->efd", up_grad, inputs, preferred_element_type=jnp.float32
    ).astype(jnp.bfloat16)
    hidden_part = jnp.einsum(
        "efr,efd->erd", gate_grad, w_gate, preferred_element_type=jnp.float32
    ) + jnp.einsum("efr,efd->erd", up_grad, w_up, preferred_element_type=jnp.float32)
    hidden_part = hidden_part.reshape(per_device, groups, shards, CAP, model_width)
    own_part = lax.psum_scatter(hidden_part, "grp", scatter_dimension=1, tiled=True)
    returned = lax.all_to_all(own_part, "shard", split_axis=2, concat_axis=2, tiled=True)
    moe_grad = jnp.einsum(
        "tesc,escd->td",
        token_map.reshape(tokens_here, per_device, shards, CAP),
        returned.reshape(per_device, shards, CAP, model_width),
        precision=lax.Precision.HIGHEST,
        preferred_element_type=jnp.float32,
    )
    input_grad = (out_grad.astype(jnp.float32) + moe_grad).astype(jnp.bfloat16)
    return (input_grad, grad_gate, grad_up, grad_down)


def solution(mesh):
    placed = (
        P(("grp", "shard"), None),
        P(("grp", "shard"), None),
        P(("grp", "shard"), None),
        P(("grp", "shard"), None),
        P("shard", "grp", None),
        P("shard", "grp", None),
        P("shard", "grp", None),
    )
    return jax.shard_map(
        body,
        mesh=mesh,
        in_specs=placed,
        out_specs=(
            P(("grp", "shard"), None),
            P("shard", "grp", None),
            P("shard", "grp", None),
            P("shard", "grp", None),
        ),
        check_vma=False,
    )
```

profile of v0, /device:TPU:0, one launch (start us, length us, event | category | flops | bytes accessed | tf_op | source)
XLA Modules:
  0.0 482.3 jit_solution(17315669654837723902)
XLA Ops:
  7.2 0.8 copy.136
  8.1 0.1 eq.51
  8.2 0.1 eq.47
  8.3 0.1 copy.138
  8.5 0.2 fusion.34
  8.8 0.2 fusion.36
  8.9 0.1 reduce_sum.21
  9.1 0.1 copy.140
  9.2 0.7 fusion.43
  9.9 0.1 convert_reduce_fusion
  10.0 1.7 convolution_convert_fusion.3
  11.7 4.1 reshape.130
  15.8 1.2 copy.149
  17.0 44.1 %all_to_all.20 = bf16[16,8,3,2048]{3,0,2,1:T(8,128)(2,1)} all-to-all(bf16[16,8,3,2048]{3,0,2,1:T(8,128)(2,1)S(1)} %copy.149), channel_id=1, replica_groups=mesh['grp'=4,'shard'=8] {'shard'}, dimensions={1} | all-to-all | bytes 3145728 | tf_op jit(solution)/shard_map/all_to_all | solution.py:51
  61.1 1.7 convolution_convert_fusion.4
  62.9 4.0 reshape.129
  66.9 1.2 copy.147
  68.0 41.0 %all_to_all.21 = bf16[16,8,3,2048]{3,0,2,1:T(8,128)(2,1)} all-to-all(bf16[16,8,3,2048]{3,0,2,1:T(8,128)(2,1)S(1)} %copy.147), channel_id=1, replica_groups=mesh['grp'=4,'shard'=8] {'shard'}, dimensions={1} | all-to-all | bytes 3145728 | tf_op jit(solution)/shard_map/all_to_all | solution.py:54
  109.0 0.0 reduce-scatter.4.cloned.1.call-start
  109.1 0.1 copy.142
  109.2 0.1 reshape.136
  109.4 0.3 convolution_reduce_fusion
  109.7 0.2 reshape.128
  109.9 0.1 copy.143
  110.0 8.0 %all_to_all.22 = bf16[16,8,3]{0,2,1:T(4,128)(2,1)S(1)} all-to-all(bf16[16,8,3]{0,2,1:T(4,128)(2,1)S(1)} %copy.143), channel_id=1, replica_groups=mesh['grp'=4,'shard'=8] {'shard'}, dimensions={1} | all-to-all | bytes 1536 | tf_op jit(solution)/shard_map/all_to_all | solution.py:57
  118.0 8.4 %all_gather.9 = bf16[16,32,3]{0,1,2:T(8,128)(2,1)S(1)} all-gather(bf16[16,8,3]{0,1,2:T(8,128)(2,1)S(1)} %copy.144), channel_id=1, replica_groups=mesh['grp'=4,'shard'=8] {'grp'}, dimensions={1}, use_global_device_ids=true | all-gather | bytes 3840 | tf_op jit(solution)/shard_map/all_gather | solution.py:68
  126.4 0.1 copy.145
  126.5 0.1 copy.146
  126.6 3.8 all-gather.5.cloned.1.call-done
  130.5 12.6 %fusion.6 = f32[16,96,192]{2,1,0:T(8,128)} fusion(bf16[16,192,2048]{2,1,0:T(8,128)(2,1)} %param.11, bf16[16,96,2048]{2,0,1:T(8,128)(2,1)} %bitcast.93), kind=kOutput, calls=%fused_computation.11 | convolution fusion | flops 1207959552 | bytes 20054016 | tf_op jit(solution)/shard_map/efd,erd->efr/dot_general | solution.py:77
  143.1 12.6 %fusion.8 = f32[16,96,192]{2,1,0:T(8,128)} fusion(bf16[16,192,2048]{2,1,0:T(8,128)(2,1)} %param.12, bf16[16,96,2048]{2,0,1:T(8,128)(2,1)} %bitcast.94), kind=kOutput, calls=%fused_computation.13 | convolution fusion | flops 1207959552 | bytes 20054016 | tf_op jit(solution)/shard_map/efd,erd->efr/dot_general | solution.py:78
  155.7 46.9 %all-gather.3.cloned.1.call-done = bf16[16,32,3,2048]{3,0,2,1:T(8,128)(2,1)} async-done(((bf16[16,8,3,2048]{3,0,2,1:T(8,128)(2,1)}), bf16[16,32,3,2048]{3,0,2,1:T(8,128)(2,1)}) %all-gather.3.cloned.1.call-update) | async-done | bytes 6291472 | tf_op jit(solution)/shard_map/all_gather | solution.py:67
  202.5 6.5 %fusion = bf16[16,96,2048]{2,0,1:T(8,128)(2,1)} fusion(bf16[16,32,3,2048]{3,0,2,1:T(8,128)(2,1)} %all-gather.3.cloned.1.call-done, f32[16,96]{0,1:T(8,128)S(1)} %reshape.134), kind=kLoop, calls=%fused_computation.1 | loop fusion | flops 9437184 | bytes 12589056 | tf_op jit(solution)/shard_map/convert_element_type | solution.py:74
  209.1 14.1 %fusion.30 = (bf16[16,192,96]{1,2,0:T(8,128)(2,1)S(1)}, bf16[16,192,96]{1,2,0:T(8,128)(2,1)}) fusion(f32[16,96,192]{2,1,0:T(8,128)} %fusion.6, f32[16,96,192]{2,1,0:T(8,128)} %fusion.8, bf16[16,192,2048]{2,1,0:T(8,128)(2,1)} %param.13, bf16[16,96,2048]{2,0,1:T(8,128)(2,1)} %fusion), kind=kOutput, calls=%fused_computation.37 | convolution fusion | flops 1211793408 | bytes 22413312 | tf_op jit(solution)/shard_map/efd,erd->efr/dot_general | solution.py:81
  223.2 6.7 %fusion.48 = f32[16,96,2048]{2,1,0:T(8,128)S(1)} fusion(bf16[16,192,96]{1,2,0:T(8,128)(2,1)} %get-tuple-element.5, bf16[16,192,2048]{2,1,0:T(8,128)(2,1)} %param.11), kind=kOutput, calls=%fused_computation.73 | convolution fusion | flops 1207959552 | bytes 25755648 | tf_op jit(solution)/shard_map/efr,efd->erd/dot_general | solution.py:93
  229.9 11.4 %convolution_add_fusion = f32[16,96,2048]{2,1,0:T(8,128)} fusion(f32[16,96,2048]{2,1,0:T(8,128)S(1)} %fusion.48, bf16[16,192,96]{1,2,0:T(8,128)(2,1)S(1)} %get-tuple-element.4, bf16[16,192,2048]{2,1,0:T(8,128)(2,1)} %param.12), kind=kOutput, calls=%fused_computation.8 | convolution fusion | flops 1211105280 | bytes 38338560 | tf_op jit(solution)/shard_map/efr,efd->erd/dot_general | solution.py:95
  241.2 16.8 %copy.152 = f32[16,96,2048]{2,0,1:T(8,128)} copy(f32[16,96,2048]{2,1,0:T(8,128)} %convolution_add_fusion) | data formatting | bytes 25165824 | tf_op jit(solution)/shard_map/add | solution.py:93
  258.0 11.5 %copy.153 = f32[16,4,8,3,2048]{4,0,2,3,1:T(8,128)} copy(f32[16,4,8,3,2048]{4,0,3,2,1:T(8,128)} %bitcast.92) | data formatting | bytes 25165824 | tf_op jit(solution)/shard_map/reshape | solution.py:96
  269.6 120.9 %reduce-scatter.4.cloned.1.call-done = f32[16,1,8,3,2048]{4,0,2,3,1:T(8,128)} async-done(((f32[16,4,8,3,2048]{4,0,2,3,1:T(8,128)}), f32[16,1,8,3,2048]{4,0,2,3,1:T(8,128)}) %reduce-scatter.4.cloned.1.call-update) | async-done | bytes 3145744
  390.5 3.9 copy.154
  394.4 4.6 all-to-all-start.3
  399.0 0.1 copy.141
  399.1 0.8 reshape.126
  399.9 16.5 %convolution_convert_fusion.1 = bf16[16,192,2048]{2,1,0:T(8,128)(2,1)} fusion(bf16[16,192,96]{1,2,0:T(8,128)(2,1)S(1)} %get-tuple-element.4, bf16[16,96,2048]{2,0,1:T(8,128)(2,1)} %bitcast.95), kind=kOutput, calls=%fused_computation.3 | convolution fusion | flops 1214251008 | bytes 19464192 | tf_op jit(solution)/shard_map/efr,erd->efd/dot_general | solution.py:90
  416.4 16.7 %convolution_convert_fusion.2 = bf16[16,192,2048]{2,1,0:T(8,128)(2,1)} fusion(bf16[16,192,96]{1,2,0:T(8,128)(2,1)S(1)} %copy-done.2, bf16[16,96,2048]{2,0,1:T(8,128)(2,1)} %bitcast.96), kind=kOutput, calls=%fused_computation.4 | convolution fusion | flops 1214251008 | bytes 19464192 | tf_op jit(solution)/shard_map/efr,erd->efd/dot_general | solution.py:87
  433.1 17.1 %convolution_convert_fusion = bf16[16,192,2048]{2,1,0:T(8,128)(2,1)} fusion(bf16[16,96,2048]{2,0,1:T(8,128)(2,1)} %fusion, f32[16,96,192]{2,1,0:T(8,128)} %fusion.8, f32[16,96,192]{2,1,0:T(8,128)S(1)} %copy-done.4), kind=kOutput, calls=%fused_computation.2 | convolution fusion | flops 1216020480 | bytes 21233664 | tf_op jit(solution)/shard_map/efr,erd->efd/dot_general | solution.py:84
  450.2 20.4 %all-to-all-done.3 = f32[16,1,8,3,2048]{4,0,3,1,2:T(8,128)} async-done(((f32[16,1,8,3,2048]{4,0,3,1,2:T(8,128)}), f32[16,1,8,3,2048]{4,0,3,1,2:T(8,128)}, u32[]{:S(2)}, u32[]{:S(2)}) %all-to-all-start.3) | async-done | bytes 3145760 | tf_op jit(solution)/shard_map/all_to_all | solution.py:98
  470.6 4.8 fusion.19
  (28 shorter events, 0.3 us)
Async XLA Ops:
  7.2 2.8 copy-start
  7.2 123.3 %all-gather.5.cloned.1.call-start = ((), (), s32[]{:S(2)}) async-start(), calls=%async_computation.6 | async-start | bytes 7864320 | tf_op jit(solution)/shard_map/all_gather | solution.py:66
  11.7 49.4 %copy-start.3 = (bf16[128,2048]{1,0:T(8,128)(2,1)S(1)}, bf16[128,2048]{1,0:T(8,128)(2,1)}, u32[]{:S(2)}) copy-start(bf16[128,2048]{1,0:T(8,128)(2,1)} %param.8) | copy-start | bytes 1572868
  61.1 141.5 %all-gather.3.cloned.1.call-start = ((), (), s32[]{:S(2)}) async-start(), calls=%async_computation.5 | async-start | bytes 7864320 | tf_op jit(solution)/shard_map/all_gather | solution.py:67
  62.8 46.2 %copy-start.6 = (bf16[128,2]{0,1:T(2,128)(2,1)S(1)}, bf16[128,2]{0,1:T(2,128)(2,1)}, u32[]{:S(2)}) copy-start(bf16[128,2]{0,1:T(2,128)(2,1)} %param.10) | copy-start | bytes 1540
  109.0 281.4 %reduce-scatter.4.cloned.1.call-start = ((), (), s32[]{:S(2)}) async-start(), calls=%async_computation.7 | async-start | bytes 15728640
  394.4 76.2 %all-to-all-start.3 = ((f32[16,1,8,3,2048]{4,0,3,1,2:T(8,128)}), f32[16,1,8,3,2048]{4,0,3,1,2:T(8,128)}, u32[]{:S(2)}, u32[]{:S(2)}) async-start(f32[16,1,8,3,2048]{4,0,3,1,2:T(8,128)} %copy.154), calls=%async_computation.3 | async-start | bytes 6291456 | tf_op jit(solution)/shard_map/all_to_all | solution.py:98
  399.9 16.5 %copy-start.2 = (bf16[16,192,96]{1,2,0:T(8,128)(2,1)S(1)}, bf16[16,192,96]{1,2,0:T(8,128)(2,1)}, u32[]{:S(2)}) copy-start(bf16[16,192,96]{1,2,0:T(8,128)(2,1)} %get-tuple-element.5) | copy-start | bytes 1769476
  416.4 16.7 %copy-start.4 = (f32[16,96,192]{2,1,0:T(8,128)S(1)}, f32[16,96,192]{2,1,0:T(8,128)}, u32[]{:S(2)}) copy-start(f32[16,96,192]{2,1,0:T(8,128)} %fusion.6) | copy-start | bytes 3538948
  433.1 37.5 %copy-start.5 = (f32[128,16,8,3]{0,3,2,1:T(4,128)S(1)}, f32[128,16,8,3]{0,3,2,1:T(4,128)}, u32[]{:S(2)}) copy-start(f32[128,16,8,3]{0,3,2,1:T(4,128)} %reshape.126) | copy-start | bytes 589828
  433.1 42.3 %copy-start.1 = (bf16[128,2048]{1,0:T(8,128)(2,1)S(1)}, bf16[128,2048]{1,0:T(8,128)(2,1)}, u32[]{:S(2)}) copy-start(bf16[128,2048]{1,0:T(8,128)(2,1)} %param.7) | copy-start | bytes 1572868
Sparse Core Ops, SparseCore 0:
  61.2 69.2 all-gather.4
  132.3 70.1 all-gather.2
  269.7 120.7 reduce-scatter.3
where the time goes:
time: 488 us; the launch traced here: 482 us
  waiting for transfers between devices  192 us (39%)
  matrix products  116 us (24%)
  blocking collectives  101 us (21%)
  local copies, waits for them, and re-layouts  45.9 us (9%)
  between operations  14.3 us (3%)
  other arithmetic  7.79 us (2%)
    unnamed x4, waiting for transfers between devices  121 us
    all_gather x1, waiting for transfers between devices, body(): lax.all_gather(arrived[1], 'grp', axis=1, tiled=True)  46.9 us
    all_to_all x1, blocking collectives, body(): lax.all_to_all(input_slots.reshape(slot_shape), 'shard', split_axis=1, co...  44.1 us
    all_to_all x1, blocking collectives, body(): lax.all_to_all(grad_slots.reshape(slot_shape), 'shard', split_axis=1, con...  41 us
    all_to_all x1, waiting for transfers between devices, body(): lax.all_to_all(own_part, 'shard', split_axis=2, concat_axis=2, tiled=True)  20.4 us
    dot_general x1, matrix products, body(): jnp.einsum('efr,erd->efd', activation, gated, preferred_element_type=jnp....  17.1 us
    add x1, local copies, waits for them, and re-layouts, body(): jnp.einsum('efr,efd->erd', gate_grad, w_gate, preferred_element_type=jnp....  16.8 us
    dot_general x1, matrix products, body(): jnp.einsum('efr,erd->efd', gate_grad, inputs, preferred_element_type=jnp....  16.7 us
  transfers between devices with their start and end apart: 4, of which 4 were waited for; matrix products, arithmetic and copies ran while one was open for 18% of the time, Pallas kernels for 0%

commit v1 on v0

v1 whole, which is shorter than its diff:
```python
import functools

import jax
import jax.numpy as jnp
from jax import lax
from jax.experimental import pallas as pl
from jax.experimental.pallas import tpu as pltpu
from jax.sharding import PartitionSpec as P

EXPERTS = 128
TOP = 2
CAP = 3
TILE = 16
PER_TILE = TILE // CAP
MESH = pl.DeviceIdType.MESH
F32 = jnp.float32
BF16 = jnp.bfloat16


def silu_parts(pre_act):
    sigmoid_val = jax.nn.sigmoid(pre_act)
    return (pre_act * sigmoid_val, sigmoid_val * (1.0 + pre_act * (1.0 - sigmoid_val)))


def flip(index, bits):
    bit = 1
    while bit <= bits:
        if bits & bit:
            index = index + bit * (1 - 2 * ((index // bit) % 2))
        bit *= 2
    return index


def places(shards):
    grp, me = lax.axis_index("grp"), lax.axis_index("shard")
    peers = [flip(me, k) for k in range(shards)]
    return grp, me, flip(grp, 1), flip(grp, 2), flip(grp, 3), peers


def greet(grp, me, grp_x, grp_y, peers):
    barrier = pltpu.get_barrier_semaphore()
    for peer in peers[1:]:
        pl.semaphore_signal(barrier, inc=1, device_id=(grp, peer), device_id_type=MESH)
    for other in (grp_x, grp_y):
        pl.semaphore_signal(barrier, inc=1, device_id=(other, me), device_id_type=MESH)
    pl.semaphore_wait(barrier, len(peers) + 1)


def remote(src, dst, send_sem, recv_sem, device):
    return pltpu.make_async_remote_copy(
        src_ref=src, dst_ref=dst, send_sem=send_sem, recv_sem=recv_sem,
        device_id=device, device_id_type=MESH,
    )


def dispatch_kernel(shards, rows_ref, out_ref, z_sem, x_sem, y_sem, fx_sem, fy_sem, own_sem):
    grp, me, grp_x, grp_y, _, peers = places(shards)
    greet(grp, me, grp_x, grp_y, peers)
    own = pltpu.make_async_copy(rows_ref.at[:, me], out_ref.at[:, grp, me], own_sem)
    own.start()

    def to_neighbours(k):
        src = rows_ref.at[:, me] if k == 0 else out_ref.at[:, grp, peers[k]]
        dst = out_ref.at[:, grp, peers[k]]
        pair = (
            remote(src, dst, x_sem.at[0, k], x_sem.at[1, k], (grp_x, me)),
            remote(src, dst, y_sem.at[0, k], y_sem.at[1, k], (grp_y, me)),
        )
        for copy in pair:
            copy.start()
        return pair

    def forward(k):
        direct[k][0].wait_recv()
        src = out_ref.at[0, grp_x, peers[k]]
        first = remote(src, src, fy_sem.at[0, k], fy_sem.at[1, k], (grp_y, me))
        first.start()
        direct[k][1].wait_recv()
        src = out_ref.at[1, grp_y, peers[k]]
        second = remote(src, src, fx_sem.at[0, k], fx_sem.at[1, k], (grp_x, me))
        second.start()
        return first, second

    direct = [to_neighbours(0)]
    over_z = [None]
    for k in range(1, shards):
        copy = remote(
            rows_ref.at[:, peers[k]], out_ref.at[:, grp, me],
            z_sem.at[0, k], z_sem.at[1, k], (grp, peers[k]),
        )
        copy.start()
        over_z.append(copy)
    passed = []
    lag = 2
    for k in range(1, shards):
        over_z[k].wait_recv()
        direct.append(to_neighbours(k))
        if k >= lag:
            passed.append(forward(k - lag))
    for k in range(shards - lag, shards):
        passed.append(forward(k))
    own.wait()
    for copy in over_z[1:]:
        copy.wait_send()
    for pair in direct:
        for copy in pair:
            copy.wait_send()
    for pair in passed:
        for copy in pair:
            copy.wait()


def dispatch(rows, groups):
    kinds, shards, depth, width = rows.shape
    sem = pltpu.SemaphoreType.DMA((2, shards))
    return pl.pallas_call(
        functools.partial(dispatch_kernel, shards),
        out_shape=jax.ShapeDtypeStruct((kinds, groups, shards, depth, width), rows.dtype),
        in_specs=[pl.BlockSpec(memory_space=pl.ANY)],
        out_specs=pl.BlockSpec(memory_space=pl.ANY),
        scratch_shapes=[sem, sem, sem, sem, sem, pltpu.SemaphoreType.DMA],
        compiler_params=pltpu.CompilerParams(collective_id=0, has_side_effects=True),
        name="dispatch",
    )(rows)


def experts_kernel(perm_ref, arrived_ref, wg_ref, wu_ref, wd_ref, gg_ref, gu_ref, gd_ref, back_ref, rows):
    step = pl.program_id(0)
    last = pl.num_programs(0) - 1
    kinds, groups, shards, depth, width = arrived_ref.shape
    tiles = depth // TILE
    half = groups // 2
    block = half * shards * TILE
    share = half * shards * CAP
    spare = half * shards
    odd = PER_TILE * tiles
    chunk = min(512, width)

    def spots(tile, side):
        spans = [(tile * PER_TILE + j, side * share, share) for j in range(PER_TILE)]
        return spans + [(odd, (2 * tile + side) * spare, spare)]

    @pl.when(step == 0)
    def _():
        def columns(c, _):
            cols = pl.ds(pl.multiple_of(c * chunk, chunk), chunk)
            for kind in range(kinds):
                for tile in range(tiles):
                    for side in range(2):
                        part = arrived_ref[
                            kind, side * half:(side + 1) * half, :, tile * TILE:(tile + 1) * TILE, cols
                        ].reshape(block, chunk)
                        sorted_part = jnp.dot(
                            perm_ref[...], part, preferred_element_type=F32
                        ).astype(BF16)
                        at = 0
                        for expert, start, size in spots(tile, side):
                            rows[kind, expert, start:start + size, cols] = sorted_part[at:at + size]
                            at += size
            return 0

        lax.fori_loop(0, width // chunk, columns, 0)

    by_last = (((1,), (1,)), ((), ()))
    by_first = (((0,), (0,)), ((), ()))
    x = rows[0, step]
    gated = rows[1, step]
    wg, wu = wg_ref[0], wu_ref[0]
    pre_gate = lax.dot_general(x, wg, by_last, preferred_element_type=F32)
    pre_up = lax.dot_general(x, wu, by_last, preferred_element_type=F32)
    act_grad = lax.dot_general(gated, wd_ref[0], by_last, preferred_element_type=F32)
    act_val, act_slope = silu_parts(pre_gate)
    activation = (act_val * pre_up).astype(BF16)
    gate_grad = (act_grad * pre_up * act_slope).astype(BF16)
    up_grad = (act_grad * act_val).astype(BF16)
    gd_ref[0] = lax.dot_general(activation, gated, by_first, preferred_element_type=F32).astype(BF16)
    gg_ref[0] = lax.dot_general(gate_grad, x, by_first, preferred_element_type=F32).astype(BF16)
    gu_ref[0] = lax.dot_general(up_grad, x, by_first, preferred_element_type=F32).astype(BF16)
    hidden = jnp.dot(gate_grad, wg, preferred_element_type=F32) + jnp.dot(
        up_grad, wu, preferred_element_type=F32
    )
    rows[0, step] = hidden.astype(BF16)

    @pl.when(step == last)
    def _():
        def columns(c, _):
            cols = pl.ds(pl.multiple_of(c * chunk, chunk), chunk)
            for tile in range(tiles):
                for side in range(2):
                    part = jnp.concatenate(
                        [rows[0, expert, start:start + size, cols] for expert, start, size in spots(tile, side)],
                        axis=0,
                    )
                    back = lax.dot_general(
                        perm_ref[...], part, by_first, preferred_element_type=F32
                    ).astype(BF16)
                    back_ref[
                        side * half:(side + 1) * half, :, tile * TILE:(tile + 1) * TILE, cols
                    ] = back.reshape(half, shards, TILE, chunk)
            return 0

        lax.fori_loop(0, width // chunk, columns, 0)


def sort_matrix(sources):
    taken = jnp.arange(sources * TILE, dtype=jnp.int32)
    source, place = taken // TILE, taken % TILE
    goes = jnp.where(
        place < PER_TILE * CAP,
        place // CAP * (sources * CAP) + source * CAP + place % CAP,
        PER_TILE * CAP * sources + source,
    )
    return (goes[None, :] == taken[:, None]).astype(BF16)


def experts(arrived, w_gate, w_up, w_down):
    kinds, groups, shards, depth, width = arrived.shape
    count, hidden, _ = w_gate.shape
    perm = sort_matrix(groups // 2 * shards)
    weight = pl.BlockSpec((1, hidden, width), lambda e: (e, 0, 0))
    grad = jax.ShapeDtypeStruct(w_gate.shape, BF16)
    row_count = groups * shards * CAP
    return pl.pallas_call(
        experts_kernel,
        grid=(count,),
        out_shape=(grad, grad, grad, jax.ShapeDtypeStruct(arrived.shape[1:], BF16)),
        in_specs=[
            pl.BlockSpec(perm.shape, lambda e: (0, 0)),
            pl.BlockSpec(arrived.shape, lambda e: (0, 0, 0, 0, 0), pipeline_mode=pl.Buffered(1)),
            weight,
            weight,
            weight,
        ],
        out_specs=(weight, weight, weight, pl.BlockSpec(arrived.shape[1:], lambda e: (0, 0, 0, 0))),
        scratch_shapes=[pltpu.VMEM((kinds, count, row_count, width), BF16)],
        compiler_params=pltpu.CompilerParams(vmem_limit_bytes=60 * 1024 * 1024),
        cost_estimate=pl.CostEstimate(
            flops=16 * count * row_count * hidden * width,
            bytes_accessed=12 * count * hidden * width + 6 * groups * shards * depth * width,
            transcendentals=count * row_count * hidden,
        ),
        name="experts",
    )(perm, arrived, w_gate, w_up, w_down)


def combine_kernel(shards, part_ref, out_ref, from_x, from_y, mid_x, mid_y, end_x, end_y, done,
                   x_sem, y_sem, x2_sem, y2_sem, z_sem):
    grp, me, grp_x, grp_y, grp_d, peers = places(shards)
    width = part_ref.shape[-1]
    low, high = pl.ds(0, width // 2), pl.ds(width // 2, width // 2)
    greet(grp, me, grp_x, grp_y, peers)
    order = list(range(shards - 1, -1, -1))

    def first(k):
        q = peers[k]
        out = []
        for j, target in enumerate((grp_d, grp_x)):
            out.append(remote(
                part_ref.at[target, q, :, low], from_x.at[q, 1 - j],
                x_sem.at[0, k, j], x_sem.at[1, k, j], (grp_x, me),
            ))
        for j, target in enumerate((grp_d, grp_y)):
            out.append(remote(
                part_ref.at[target, q, :, high], from_y.at[q, 1 - j],
                y_sem.at[0, k, j], y_sem.at[1, k, j], (grp_y, me),
            ))
        for copy in (out[0], out[2], out[1], out[3]):
            copy.start()
        return out

    def second(k):
        q = peers[k]
        starts[k][0].wait_recv()
        mid_x[q] = (part_ref[grp_y, q, :, low].astype(F32) + from_x[q, 1].astype(F32)).astype(BF16)
        to_y = remote(mid_x.at[q], end_y.at[q], y2_sem.at[0, k], y2_sem.at[1, k], (grp_y, me))
        to_y.start()
        starts[k][2].wait_recv()
        mid_y[q] = (part_ref[grp_x, q, :, high].astype(F32) + from_y[q, 1].astype(F32)).astype(BF16)
        to_x = remote(mid_y.at[q], end_x.at[q], x2_sem.at[0, k], x2_sem.at[1, k], (grp_x, me))
        to_x.start()
        return to_y, to_x

    def third(k):
        q = peers[k]
        starts[k][1].wait_recv()
        middles[k][0].wait_recv()
        done[q, :, low] = (
            part_ref[grp, q, :, low].astype(F32) + from_x[q, 0].astype(F32) + end_y[q].astype(F32)
        ).astype(BF16)
        starts[k][3].wait_recv()
        middles[k][1].wait_recv()
        done[q, :, high] = (
            part_ref[grp, q, :, high].astype(F32) + from_y[q, 0].astype(F32) + end_x[q].astype(F32)
        ).astype(BF16)
        if k == 0:
            out_ref[me] = done[me]
            return None
        copy = remote(done.at[q], out_ref.at[me], z_sem.at[0, k], z_sem.at[1, k], (grp, q))
        copy.start()
        return copy

    starts, middles, returns = {}, {}, []
    ahead, lag = 2, 1
    for i in range(shards + ahead + lag):
        if i < shards:
            starts[order[i]] = first(order[i])
        if 0 <= i - ahead < shards:
            middles[order[i - ahead]] = second(order[i - ahead])
        if 0 <= i - ahead - lag:
            returns.append(third(order[i - ahead - lag]))
    for k in order:
        for copy in starts[k]:
            copy.wait_send()
        for copy in middles[k]:
            copy.wait_send()
    for copy in returns:
        if copy is not None:
            copy.wait()


def combine(parts):
    groups, shards, depth, width = parts.shape
    half = (shards, depth, width // 2)
    pair = (shards, 2, depth, width // 2)
    return pl.pallas_call(
        functools.partial(combine_kernel, shards),
        out_shape=jax.ShapeDtypeStruct((shards, depth, width), parts.dtype),
        in_specs=[pl.BlockSpec(memory_space=pltpu.VMEM)],
        out_specs=pl.BlockSpec(memory_space=pltpu.VMEM),
        scratch_shapes=[
            pltpu.VMEM(pair, BF16), pltpu.VMEM(pair, BF16),
            pltpu.VMEM(half, BF16), pltpu.VMEM(half, BF16),
            pltpu.VMEM(half, BF16), pltpu.VMEM(half, BF16),
            pltpu.VMEM((shards, depth, width), BF16),
            pltpu.SemaphoreType.DMA((2, shards, 2)), pltpu.SemaphoreType.DMA((2, shards, 2)),
            pltpu.SemaphoreType.DMA((2, shards)), pltpu.SemaphoreType.DMA((2, shards)),
            pltpu.SemaphoreType.DMA((2, shards)),
        ],
        compiler_params=pltpu.CompilerParams(
            collective_id=1, has_side_effects=True, vmem_limit_bytes=48 * 1024 * 1024
        ),
        name="combine",
    )(parts)


def body(moe_input, out_grad, expert_ids, gate_weights, w_gate, w_up, w_down):
    contract_rows = (((0,), (0,)), ((), ()))
    shards = lax.axis_size("shard")
    groups = lax.axis_size("grp")
    per_device = w_gate.shape[0]
    tokens_here, model_width = moe_input.shape
    depth = per_device * CAP
    tiles = depth // TILE
    flat_ids = expert_ids.reshape(tokens_here * TOP)
    matches = (flat_ids[:, None] == jnp.arange(EXPERTS, dtype=jnp.int32)[None, :]).astype(jnp.int32)
    rank_of = jnp.sum((jnp.cumsum(matches, axis=0) - matches) * matches, axis=1)
    local = flat_ids % per_device
    odd = PER_TILE * tiles
    place = jnp.where(
        local < odd,
        local // PER_TILE * TILE + local % PER_TILE * CAP + rank_of,
        rank_of * TILE + PER_TILE * CAP,
    )
    slot_of = (flat_ids // per_device * depth + place).reshape(tokens_here, TOP)
    slots = jnp.arange(EXPERTS * CAP, dtype=jnp.int32)
    chosen = slot_of[:, :, None] == slots[None, None, :]
    token_map = jnp.any(chosen, axis=1).astype(BF16)
    gate_map = jnp.sum(
        jnp.where(chosen, gate_weights.astype(F32)[:, :, None], 0.0), axis=1
    ).astype(BF16)
    input_slots = lax.dot_general(token_map, moe_input, contract_rows, preferred_element_type=F32)
    gated_slots = lax.dot_general(gate_map, out_grad, contract_rows, preferred_element_type=F32)
    sent = jnp.stack([input_slots.astype(BF16), gated_slots.astype(BF16)])
    arrived = dispatch(sent.reshape(2, shards, depth, model_width), groups)
    grad_gate, grad_up, grad_down, parts = experts(arrived, w_gate, w_up, w_down)
    returned = combine(parts).reshape(shards * depth, model_width)
    moe_grad = jnp.dot(token_map, returned, preferred_element_type=F32)
    input_grad = (out_grad.astype(F32) + moe_grad).astype(BF16)
    return (input_grad, grad_gate, grad_up, grad_down)


def plain_slot_maps(ids_here, per_device, shards):
    tokens_here = ids_here.shape[0]
    flat_ids = ids_here.reshape(tokens_here * TOP)
    matches = (flat_ids[:, None] == jnp.arange(EXPERTS, dtype=jnp.int32)[None, :]).astype(jnp.int32)
    rank_of = jnp.sum((jnp.cumsum(matches, axis=0) - matches) * matches, axis=1)
    slot_of = flat_ids % per_device * (shards * CAP) + flat_ids // per_device * CAP + rank_of
    return (slot_of[:, None] == jnp.arange(EXPERTS * CAP, dtype=jnp.int32)[None, :]).astype(F32)


def plain_body(moe_input, out_grad, expert_ids, gate_weights, w_gate, w_up, w_down):
    contract_rows = (((0,), (0,)), ((), ()))
    shards = lax.axis_size("shard")
    groups = lax.axis_size("grp")
    per_device = w_gate.shape[0]
    tokens_here, model_width = moe_input.shape
    slot_total = EXPERTS * CAP
    chosen = plain_slot_maps(expert_ids, per_device, shards).reshape(tokens_here, TOP, slot_total)
    token_map = jnp.sum(chosen, axis=1)
    gate_map = jnp.sum(chosen * gate_weights.astype(F32)[:, :, None], axis=1).astype(BF16)
    slot_shape = (per_device, shards, CAP, model_width)
    row_count = groups * shards * CAP

    def send(mapping, rows):
        slots = lax.dot_general(mapping, rows, contract_rows, preferred_element_type=F32).astype(BF16)
        arrived = lax.all_to_all(
            slots.reshape(slot_shape), "shard", split_axis=1, concat_axis=1, tiled=True
        )
        gathered = lax.all_gather(arrived, "grp", axis=1, tiled=True)
        return gathered.reshape(per_device, row_count, model_width)

    inputs = send(token_map.astype(BF16), moe_input)
    gated = send(gate_map, out_grad)
    pre_gate = jnp.einsum("efd,erd->efr", w_gate, inputs, preferred_element_type=F32)
    pre_up = jnp.einsum("efd,erd->efr", w_up, inputs, preferred_element_type=F32)
    act_val, act_slope = silu_parts(pre_gate)
    activation = (act_val * pre_up).astype(BF16)
    act_grad = jnp.einsum("efd,erd->efr", w_down, gated, preferred_element_type=F32)
    gate_grad = (act_grad * pre_up * act_slope).astype(BF16)
    up_grad = (act_grad * act_val).astype(BF16)
    grad_down = jnp.einsum("efr,erd->efd", activation, gated, preferred_element_type=F32).astype(BF16)
    grad_gate = jnp.einsum("efr,erd->efd", gate_grad, inputs, preferred_element_type=F32).astype(BF16)
    grad_up = jnp.einsum("efr,erd->efd", up_grad, inputs, preferred_element_type=F32).astype(BF16)
    hidden_part = jnp.einsum(
        "efr,efd->erd", gate_grad, w_gate, preferred_element_type=F32
    ) + jnp.einsum("efr,efd->erd", up_grad, w_up, preferred_element_type=F32)
    hidden_part = hidden_part.reshape(per_device, groups, shards, CAP, model_width)
    own_part = lax.psum_scatter(hidden_part, "grp", scatter_dimension=1, tiled=True)
    returned = lax.all_to_all(own_part, "shard", split_axis=2, concat_axis=2, tiled=True)
    moe_grad = jnp.einsum(
        "tesc,escd->td",
        token_map.reshape(tokens_here, per_device, shards, CAP),
        returned.reshape(per_device, shards, CAP, model_width),
        precision=lax.Precision.HIGHEST,
        preferred_element_type=F32,
    )
    input_grad = (out_grad.astype(F32) + moe_grad).astype(BF16)
    return (input_grad, grad_gate, grad_up, grad_down)


def solution(mesh):
    groups, shards = mesh.shape["grp"], mesh.shape["shard"]
    per_device = EXPERTS // shards
    tiles = per_device * CAP // TILE
    fits = (
        groups == 4
        and shards & (shards - 1) == 0
        and per_device * CAP == tiles * TILE
        and per_device == PER_TILE * tiles + 1
        and tiles == CAP
    )
    tokens = P(("grp", "shard"), None)
    weights = P("shard", "grp", None)
    return jax.shard_map(
        body if fits else plain_body,
        mesh=mesh,
        in_specs=(tokens, tokens, tokens, tokens, weights, weights, weights),
        out_specs=(tokens, weights, weights, weights),
        check_vma=False,
    )
```

time: 488 us -> 247 us (0.51)
  Pallas kernels: 0 us -> 236 us
  waiting for transfers between devices: 192 us -> 0 us
  matrix products: 116 us -> 3.49 us
  blocking collectives: 101 us -> 0 us
  local copies, waits for them, and re-layouts: 45.9 us -> 1.43 us
  between operations: 14.3 us -> 0.76 us
    pallas_call x0 -> x3, Pallas kernels: none -> 236 us  [the longest x1 120 us: dispatch(): pl.pallas_call(functools.partial(dispatch_kernel, shards), out_shape=jax....]
    unnamed x4 -> x0, waiting for transfers between devices: 121 us -> none
    dot_general x12 -> x3, matrix products: 116 us -> 3.49 us  [the longest x1 1.63 us: body(): lax.dot_general(gate_map, out_grad, contract_rows, preferred_element_type...]
    all_to_all x3 -> x0, blocking collectives: 93 us -> none  [the longest x1 44.1 us: body(): lax.all_to_all(input_slots.reshape(slot_shape), 'shard', split_axis=1, co...]
    all_gather x2 -> x0, waiting for transfers between devices: 50.7 us -> none  [the longest x1 46.9 us: body(): lax.all_gather(arrived[1], 'grp', axis=1, tiled=True)]
    reshape x9 -> x0, local copies, waits for them, and re-layouts: 23.3 us -> none  [the longest x1 11.5 us: body(): hidden_part.reshape(per_device, groups, shards, CAP, model_width)]
    all_to_all x1 -> x0, waiting for transfers between devices: 20.4 us -> none  [body(): lax.all_to_all(own_part, 'shard', split_axis=2, concat_axis=2, tiled=True)]
    add x1 -> x0, local copies, waits for them, and re-layouts: 16.8 us -> none  [body(): jnp.einsum('efr,efd->erd', gate_grad, w_gate, preferred_element_type=jnp....]
  transfers between devices with their start and end apart: 4 -> 0, of which waited for: 4 -> 0; matrix products, arithmetic and copies ran while one was open for 18% -> 0% of each run, Pallas kernels for 0% -> 0%
where the time goes in v1:
time: 247 us; the launch traced here: 246 us
  Pallas kernels  236 us (96%)
  other arithmetic  4.75 us (2%)
  matrix products  3.49 us (1%)
    pallas_call x1, Pallas kernels, dispatch(): pl.pallas_call(functools.partial(dispatch_kernel, shards), out_shape=jax....  120 us
    pallas_call x1, Pallas kernels, combine(): pl.pallas_call(functools.partial(combine_kernel, shards), out_shape=jax.S...  65.5 us
    pallas_call x1, Pallas kernels, experts(): pl.pallas_call(experts_kernel, grid=(count,), out_shape=(grad, grad, grad...  50.2 us

profile of v1, /device:TPU:0, one launch (start us, length us, event | category | flops | bytes accessed | tf_op | source)
XLA Modules:
  0.0 246.1 jit_solution(10937875733196467479)
XLA Ops:
  0.6 0.0 copy-start
  0.6 0.7 convert_element_type.34
  1.4 0.8 copy.37
  2.2 0.1 eq.60
  2.3 0.1 eq.56
  2.4 0.1 copy.39
  2.6 0.2 fusion.3
  2.9 0.2 fusion.5
  3.0 0.1 reduce_sum.21
  3.2 0.1 copy.41
  3.3 0.7 fusion.11
  4.0 0.1 fusion.1
  4.1 0.1 select_reduce_fusion
  4.2 0.7 fusion.2.perm_ref
  4.9 1.6 convolution_convert_fusion
  6.6 0.0 copy-done
  6.6 0.6 convolution_convert_fusion.1
  7.2 1.9 pad_maximum_fusion.rows_ref
  9.1 119.9 %dispatch.1.arrived_ref = bf16[2,4,8,48,2048]{4,3,2,1,0:T(8,128)(2,1)} custom-call(bf16[2,8,48,2048]{3,2,1,0:T(8,128)(2,1)} %pad_maximum_fusion.rows_ref), custom_call_target="tpu_custom_call" | custom-call | tf_op jit(solution)/shard_map/dispatch/pallas_call | solution.py:116
  129.1 50.2 %experts.1 = (bf16[16,192,2048]{2,1,0:T(8,128)(2,1)}, bf16[16,192,2048]{2,1,0:T(8,128)(2,1)}, bf16[16,192,2048]{2,1,0:T(8,128)(2,1)}, bf16[4,8,48,2048]{3,2,1,0:T(8,128)(2,1)}) custom-call(bf16[256,256]{1,0:T(8,128)(2,1)} %fusion.2.perm_ref, bf16[2,4,8,48,2048]{4,3,2,1,0:T(8,128)(2,1)} %dispatch.1.arrived_ref, bf16[16,192,2048]{2,1,0:T(8,128)(2,1)} %wg_ref.1, ...), custom_call_target="tpu_custom_call" | custom-call | flops 9663676416 | bytes 94371840 | tf_op jit(solution)/shard_map/experts/pallas_call | solution.py:223
  179.3 0.0 copy-start.2
  179.3 0.0 copy-start.1
  179.3 65.5 %combine.1 = bf16[8,48,2048]{2,1,0:T(8,128)(2,1)S(1)} custom-call(bf16[4,8,48,2048]{3,2,1,0:T(8,128)(2,1)} %get-tuple-element.8.part_ref), custom_call_target="tpu_custom_call" | custom-call | tf_op jit(solution)/shard_map/combine/pallas_call | solution.py:325
  244.8 0.0 copy-done.2
  244.8 1.2 fusion
  246.1 0.0 copy-done.1
  (7 shorter events, 0.1 us)
Async XLA Ops:
  0.6 5.9 %copy-start = (bf16[128,2048]{1,0:T(8,128)(2,1)S(1)}, bf16[128,2048]{1,0:T(8,128)(2,1)}, u32[]{:S(2)}) copy-start(bf16[128,2048]{1,0:T(8,128)(2,1)} %param.7) | copy-start | bytes 1572868
  179.3 65.5 %copy-start.2 = (bf16[128,2048]{1,0:T(8,128)(2,1)S(1)}, bf16[128,2048]{1,0:T(8,128)(2,1)}, u32[]{:S(2)}) copy-start(bf16[128,2048]{1,0:T(8,128)(2,1)} %param.8) | copy-start | bytes 1572868
  179.3 66.8 %copy-start.1 = (bf16[128,2048]{1,0:T(8,128)(2,1)S(1)}, bf16[128,2048]{1,0:T(8,128)(2,1)}, u32[]{:S(2)}) copy-start(bf16[128,2048]{1,0:T(8,128)(2,1)} %param.7) | copy-start | bytes 1572868

commit v2 on v0

v2 whole, which is shorter than its diff:
```python
import functools

import jax
import jax.numpy as jnp
from jax import lax
from jax.experimental import pallas as pl
from jax.experimental.pallas import tpu as pltpu
from jax.sharding import PartitionSpec as P

EXPERTS = 128
TOP = 2
CAP = 3
TILE = 16
PER_TILE = TILE // CAP
MESH = pl.DeviceIdType.MESH
F32 = jnp.float32
BF16 = jnp.bfloat16


def silu_parts(pre_act):
    sigmoid_val = jax.nn.sigmoid(pre_act)
    return (pre_act * sigmoid_val, sigmoid_val * (1.0 + pre_act * (1.0 - sigmoid_val)))


def flip(index, bits):
    bit = 1
    while bit <= bits:
        if bits & bit:
            index = index + bit * (1 - 2 * ((index // bit) % 2))
        bit *= 2
    return index


def places(shards):
    grp, me = lax.axis_index("grp"), lax.axis_index("shard")
    peers = [flip(me, k) for k in range(shards)]
    return grp, me, flip(grp, 1), flip(grp, 2), flip(grp, 3), peers


def greet(grp, me, grp_x, grp_y, peers):
    barrier = pltpu.get_barrier_semaphore()
    for peer in peers[1:]:
        pl.semaphore_signal(barrier, inc=1, device_id=(grp, peer), device_id_type=MESH)
    for other in (grp_x, grp_y):
        pl.semaphore_signal(barrier, inc=1, device_id=(other, me), device_id_type=MESH)
    pl.semaphore_wait(barrier, len(peers) + 1)


def remote(src, dst, send_sem, recv_sem, device):
    return pltpu.make_async_remote_copy(
        src_ref=src, dst_ref=dst, send_sem=send_sem, recv_sem=recv_sem,
        device_id=device, device_id_type=MESH,
    )


def exchange_kernel(order, rows_ref, wg_ref, wu_ref, wd_ref, perm_ref, sorted_ref, acts_ref, out_ref,
                    arrived, rows, hidden, parts, weights, from_x, from_y, mid_x, mid_y, end_x, end_y, done,
                    zs, xs, ys, fxs, fys, cx, cy, cx2, cy2, cz, w_sem, own_sem, sorted_sem):
    shards = len(order)
    grp, me, grp_x, grp_y, _, by_flip = places(shards)
    peers = [by_flip[k] for k in order]
    kinds, groups, _, depth, width = arrived.shape
    count = rows.shape[1]
    tiles = depth // TILE
    half = shards // 2
    block = groups * half * TILE
    share = groups * half * CAP
    spare = groups * half
    odd = PER_TILE * tiles
    chunk = min(512, width)
    low, high = pl.ds(0, width // 2), pl.ds(width // 2, width // 2)
    by_last = (((1,), (1,)), ((), ()))
    by_first = (((0,), (0,)), ((), ()))
    on_x, on_y = (grp_x, me), (grp_y, me)

    def weight_copies(e, slot):
        return [
            pltpu.make_async_copy(ref.at[e], weights.at[j, slot], w_sem.at[j, slot])
            for j, ref in enumerate((wg_ref, wu_ref, wd_ref))
        ]

    def to_neighbours(i):
        src = rows_ref.at[:, me] if i == 0 else arrived.at[:, 0, i]
        pair = (
            remote(src, arrived.at[:, 1, i], xs.at[0, i], xs.at[1, i], on_x),
            remote(src, arrived.at[:, 2, i], ys.at[0, i], ys.at[1, i], on_y),
        )
        for copy in pair:
            copy.start()
        direct[i] = pair

    def forward(i):
        direct[i][0].wait_recv()
        first = remote(arrived.at[0, 1, i], arrived.at[0, 3, i], fys.at[0, i], fys.at[1, i], on_y)
        first.start()
        direct[i][1].wait_recv()
        second = remote(arrived.at[1, 2, i], arrived.at[1, 3, i], fxs.at[0, i], fxs.at[1, i], on_x)
        second.start()
        passed[i] = (first, second)

    def relay(i):
        over_z[i].wait_recv()
        to_neighbours(i)
        if i >= 2:
            forward(i - 2)

    def sort(side):
        for i in range(side * half, (side + 1) * half):
            for copy in passed[i]:
                copy.wait_recv()

        def columns(c, _):
            cols = pl.ds(pl.multiple_of(c * chunk, chunk), chunk)
            for kind in range(kinds):
                for tile in range(tiles):
                    part = arrived[
                        kind, :, side * half:(side + 1) * half, tile * TILE:(tile + 1) * TILE, cols
                    ].reshape(block, chunk)
                    placed = jnp.dot(perm_ref[...], part, preferred_element_type=F32).astype(BF16)
                    base = side * share
                    for j in range(PER_TILE):
                        rows[kind, tile * PER_TILE + j, base:base + share, cols] = placed[j * share:(j + 1) * share]
                    base += tile * spare
                    rows[kind, odd, base:base + spare, cols] = placed[PER_TILE * share:]
            return 0

        lax.fori_loop(0, width // chunk, columns, 0)
        span = pl.ds(side * share, share)
        copy = pltpu.make_async_copy(rows.at[:, :, span], sorted_ref.at[:, :, span], sorted_sem.at[side])
        copy.start()
        written.append(copy)

    def experts(side, begin, end):
        span = pl.ds(side * share, share)

        def one(e, _):
            slot = e % 2

            def fetch():
                for copy in weight_copies((e + 1) % count, 1 - slot):
                    copy.start()

            if side == 0:
                fetch()
            else:
                pl.when(e + 1 < count)(fetch)
            for copy in weight_copies(e, slot):
                copy.wait()
            x = rows[0, e, span]
            gated = rows[1, e, span]
            wg, wu = weights[0, slot], weights[1, slot]
            pre_gate = lax.dot_general(x, wg, by_last, preferred_element_type=F32)
            pre_up = lax.dot_general(x, wu, by_last, preferred_element_type=F32)
            act_grad = lax.dot_general(gated, weights[2, slot], by_last, preferred_element_type=F32)
            act_val, act_slope = silu_parts(pre_gate)
            gate_grad = (act_grad * pre_up * act_slope).astype(BF16)
            up_grad = (act_grad * act_val).astype(BF16)
            acts_ref[0, e, span] = (act_val * pre_up).astype(BF16)
            acts_ref[1, e, span] = gate_grad
            acts_ref[2, e, span] = up_grad
            hidden[e] = (
                jnp.dot(gate_grad, wg, preferred_element_type=F32)
                + jnp.dot(up_grad, wu, preferred_element_type=F32)
            ).astype(BF16)
            return 0

        lax.fori_loop(begin, end, one, 0)

    def unsort(side):
        def columns(c, _):
            cols = pl.ds(pl.multiple_of(c * chunk, chunk), chunk)
            for tile in range(tiles):
                spans = [hidden[tile * PER_TILE + j, :, cols] for j in range(PER_TILE)]
                spans.append(hidden[odd, tile * spare:(tile + 1) * spare, cols])
                back = lax.dot_general(
                    perm_ref[...], jnp.concatenate(spans, axis=0), by_first, preferred_element_type=F32
                ).astype(BF16)
                parts[
                    :, side * half:(side + 1) * half, tile * TILE:(tile + 1) * TILE, cols
                ] = back.reshape(groups, half, TILE, chunk)
            return 0

        lax.fori_loop(0, width // chunk, columns, 0)

    def first(i):
        out = []
        for j, rel in enumerate((3, 1)):
            out.append(remote(
                parts.at[rel, i, :, low], from_x.at[i, 1 - j], cx.at[0, i, j], cx.at[1, i, j], on_x
            ))
        for j, rel in enumerate((3, 2)):
            out.append(remote(
                parts.at[rel, i, :, high], from_y.at[i, 1 - j], cy.at[0, i, j], cy.at[1, i, j], on_y
            ))
        for copy in (out[0], out[2], out[1], out[3]):
            copy.start()
        starts[i] = out

    def second(i):
        starts[i][0].wait_recv()
        mid_x[i] = (parts[2, i, :, low].astype(F32) + from_x[i, 1].astype(F32)).astype(BF16)
        to_y = remote(mid_x.at[i], end_y.at[i], cy2.at[0, i], cy2.at[1, i], on_y)
        to_y.start()
        starts[i][2].wait_recv()
        mid_y[i] = (parts[1, i, :, high].astype(F32) + from_y[i, 1].astype(F32)).astype(BF16)
        to_x = remote(mid_y.at[i], end_x.at[i], cx2.at[0, i], cx2.at[1, i], on_x)
        to_x.start()
        middles[i] = (to_y, to_x)

    def third(i):
        starts[i][1].wait_recv()
        middles[i][0].wait_recv()
        done[i, :, low] = (
            parts[0, i, :, low].astype(F32) + from_x[i, 0].astype(F32) + end_y[i].astype(F32)
        ).astype(BF16)
        starts[i][3].wait_recv()
        middles[i][1].wait_recv()
        done[i, :, high] = (
            parts[0, i, :, high].astype(F32) + from_y[i, 0].astype(F32) + end_x[i].astype(F32)
        ).astype(BF16)
        if i == 0:
            out_ref[me] = done[0]
            return
        copy = remote(done.at[i], out_ref.at[me], cz.at[0, i], cz.at[1, i], (grp, peers[i]))
        copy.start()
        returns.append(copy)

    direct, over_z, passed, starts, middles = {}, {}, {}, {}, {}
    returns, written = [], []
    for copy in weight_copies(0, 0):
        copy.start()
    greet(grp, me, grp_x, grp_y, by_flip)
    own = pltpu.make_async_copy(rows_ref.at[:, me], arrived.at[:, 0, 0], own_sem)
    own.start()
    to_neighbours(0)
    for i in range(1, shards):
        over_z[i] = remote(
            rows_ref.at[:, peers[i]], arrived.at[:, 0, i], zs.at[0, i], zs.at[1, i], (grp, peers[i])
        )
        over_z[i].start()
    for i in range(1, half + 2):
        relay(i)
    own.wait()
    sort(0)
    steps = half - 2
    for j, i in enumerate(range(half + 2, shards)):
        relay(i)
        experts(0, j * count // steps, (j + 1) * count // steps)
    forward(shards - 2)
    unsort(0)
    turn = list(range(half // 2, half)) + list(range(half // 2 - 1, -1, -1))
    first(turn[0])
    first(turn[1])
    forward(shards - 1)
    for i in turn[2:]:
        first(i)
    sort(1)
    for j, i in enumerate(turn):
        experts(1, j * count // half, (j + 1) * count // half)
        second(i)
        if j > 0:
            third(turn[j - 1])
    unsort(1)
    later = [half + i for i in turn]
    ahead = 2
    for j in range(half + ahead + 1):
        if j < half:
            first(later[j])
        if j == 1:
            third(turn[-1])
        if 0 <= j - ahead < half:
            second(later[j - ahead])
        if 0 <= j - ahead - 1:
            third(later[j - ahead - 1])
    for i in range(shards):
        if i > 0:
            over_z[i].wait_send()
        for copy in direct[i] + passed[i] + tuple(starts[i]) + middles[i]:
            copy.wait_send()
    for copy in written:
        copy.wait()
    for copy in returns:
        copy.wait()


def sort_matrix(sources):
    taken = jnp.arange(sources * TILE, dtype=jnp.int32)
    source, place = taken // TILE, taken % TILE
    goes = jnp.where(
        place < PER_TILE * CAP,
        place // CAP * (sources * CAP) + source * CAP + place % CAP,
        PER_TILE * CAP * sources + source,
    )
    return (goes[None, :] == taken[:, None]).astype(BF16)


def exchange(sent, w_gate, w_up, w_down, groups):
    kinds, shards, depth, width = sent.shape
    count, units, _ = w_gate.shape
    row_count = groups * shards * CAP
    order = sorted(range(shards), key=lambda k: (k // 2 % 2, k))
    perm = sort_matrix(groups * shards // 2)
    half = pltpu.VMEM((shards, depth, width // 2), BF16)
    pair = pltpu.VMEM((shards, 2, depth, width // 2), BF16)
    sem = pltpu.SemaphoreType.DMA((2, shards))
    sem_pair = pltpu.SemaphoreType.DMA((2, shards, 2))
    anywhere = pl.BlockSpec(memory_space=pl.ANY)
    near = pl.BlockSpec(memory_space=pltpu.VMEM)
    return pl.pallas_call(
        functools.partial(exchange_kernel, order),
        out_shape=(
            jax.ShapeDtypeStruct((kinds, count, row_count, width), BF16),
            jax.ShapeDtypeStruct((3, count, row_count, units), BF16),
            jax.ShapeDtypeStruct((shards, depth, width), BF16),
        ),
        in_specs=[anywhere, anywhere, anywhere, anywhere, near],
        out_specs=(anywhere, near, near),
        scratch_shapes=[
            pltpu.VMEM((kinds, groups, shards, depth, width), BF16),
            pltpu.VMEM((kinds, count, row_count, width), BF16),
            pltpu.VMEM((count, row_count // 2, width), BF16),
            pltpu.VMEM((groups, shards, depth, width), BF16),
            pltpu.VMEM((3, 2, units, width), BF16),
            pair, pair, half, half, half, half,
            pltpu.VMEM((shards, depth, width), BF16),
            sem, sem, sem, sem, sem, sem_pair, sem_pair, sem, sem, sem,
            pltpu.SemaphoreType.DMA((3, 2)),
            pltpu.SemaphoreType.DMA,
            pltpu.SemaphoreType.DMA((2,)),
        ],
        compiler_params=pltpu.CompilerParams(
            collective_id=0, has_side_effects=True, vmem_limit_bytes=60 * 1024 * 1024
        ),
        name="exchange",
    )(sent, w_gate, w_up, w_down, perm)


def grads_kernel(rows_ref, acts_ref, gg_ref, gu_ref, gd_ref):
    by_first = (((0,), (0,)), ((), ()))
    x, gated = rows_ref[0, 0], rows_ref[1, 0]
    for ref, j, side in ((gd_ref, 0, gated), (gg_ref, 1, x), (gu_ref, 2, x)):
        ref[0] = lax.dot_general(acts_ref[j, 0], side, by_first, preferred_element_type=F32).astype(BF16)


def grads(rows, acts):
    kinds, count, row_count, width = rows.shape
    units = acts.shape[-1]
    grad = jax.ShapeDtypeStruct((count, units, width), BF16)
    out = pl.BlockSpec((1, units, width), lambda e: (e, 0, 0))
    return pl.pallas_call(
        grads_kernel,
        grid=(count,),
        out_shape=(grad, grad, grad),
        in_specs=[
            pl.BlockSpec((kinds, 1, row_count, width), lambda e: (0, e, 0, 0)),
            pl.BlockSpec((3, 1, row_count, units), lambda e: (0, e, 0, 0)),
        ],
        out_specs=(out, out, out),
        compiler_params=pltpu.CompilerParams(vmem_limit_bytes=32 * 1024 * 1024),
        name="grads",
    )(rows, acts)


def body(moe_input, out_grad, expert_ids, gate_weights, w_gate, w_up, w_down):
    contract_rows = (((0,), (0,)), ((), ()))
    shards = lax.axis_size("shard")
    groups = lax.axis_size("grp")
    per_device = w_gate.shape[0]
    tokens_here, model_width = moe_input.shape
    depth = per_device * CAP
    tiles = depth // TILE
    flat_ids = expert_ids.reshape(tokens_here * TOP)
    matches = (flat_ids[:, None] == jnp.arange(EXPERTS, dtype=jnp.int32)[None, :]).astype(jnp.int32)
    rank_of = jnp.sum((jnp.cumsum(matches, axis=0) - matches) * matches, axis=1)
    local = flat_ids % per_device
    odd = PER_TILE * tiles
    place = jnp.where(
        local < odd,
        local // PER_TILE * TILE + local % PER_TILE * CAP + rank_of,
        rank_of * TILE + PER_TILE * CAP,
    )
    slot_of = (flat_ids // per_device * depth + place).reshape(tokens_here, TOP)
    slots = jnp.arange(EXPERTS * CAP, dtype=jnp.int32)
    chosen = slot_of[:, :, None] == slots[None, None, :]
    token_map = jnp.any(chosen, axis=1).astype(BF16)
    gate_map = jnp.sum(
        jnp.where(chosen, gate_weights.astype(F32)[:, :, None], 0.0), axis=1
    ).astype(BF16)
    input_slots = lax.dot_general(token_map, moe_input, contract_rows, preferred_element_type=F32)
    gated_slots = lax.dot_general(gate_map, out_grad, contract_rows, preferred_element_type=F32)
    sent = jnp.stack([input_slots.astype(BF16), gated_slots.astype(BF16)])
    sorted_rows, acts, returned = exchange(
        sent.reshape(2, shards, depth, model_width), w_gate, w_up, w_down, groups
    )
    grad_gate, grad_up, grad_down = grads(sorted_rows, acts)
    returned = returned.reshape(shards * depth, model_width)
    moe_grad = jnp.dot(token_map, returned, preferred_element_type=F32)
    input_grad = (out_grad.astype(F32) + moe_grad).astype(BF16)
    return (input_grad, grad_gate, grad_up, grad_down)


def plain_slot_maps(ids_here, per_device, shards):
    tokens_here = ids_here.shape[0]
    flat_ids = ids_here.reshape(tokens_here * TOP)
    matches = (flat_ids[:, None] == jnp.arange(EXPERTS, dtype=jnp.int32)[None, :]).astype(jnp.int32)
    rank_of = jnp.sum((jnp.cumsum(matches, axis=0) - matches) * matches, axis=1)
    slot_of = flat_ids % per_device * (shards * CAP) + flat_ids // per_device * CAP + rank_of
    return (slot_of[:, None] == jnp.arange(EXPERTS * CAP, dtype=jnp.int32)[None, :]).astype(F32)


def plain_body(moe_input, out_grad, expert_ids, gate_weights, w_gate, w_up, w_down):
    contract_rows = (((0,), (0,)), ((), ()))
    shards = lax.axis_size("shard")
    groups = lax.axis_size("grp")
    per_device = w_gate.shape[0]
    tokens_here, model_width = moe_input.shape
    slot_total = EXPERTS * CAP
    chosen = plain_slot_maps(expert_ids, per_device, shards).reshape(tokens_here, TOP, slot_total)
    token_map = jnp.sum(chosen, axis=1)
    gate_map = jnp.sum(chosen * gate_weights.astype(F32)[:, :, None], axis=1).astype(BF16)
    slot_shape = (per_device, shards, CAP, model_width)
    row_count = groups * shards * CAP

    def send(mapping, rows):
        slots = lax.dot_general(mapping, rows, contract_rows, preferred_element_type=F32).astype(BF16)
        arrived = lax.all_to_all(
            slots.reshape(slot_shape), "shard", split_axis=1, concat_axis=1, tiled=True
        )
        gathered = lax.all_gather(arrived, "grp", axis=1, tiled=True)
        return gathered.reshape(per_device, row_count, model_width)

    inputs = send(token_map.astype(BF16), moe_input)
    gated = send(gate_map, out_grad)
    pre_gate = jnp.einsum("efd,erd->efr", w_gate, inputs, preferred_element_type=F32)
    pre_up = jnp.einsum("efd,erd->efr", w_up, inputs, preferred_element_type=F32)
    act_val, act_slope = silu_parts(pre_gate)
    activation = (act_val * pre_up).astype(BF16)
    act_grad = jnp.einsum("efd,erd->efr", w_down, gated, preferred_element_type=F32)
    gate_grad = (act_grad * pre_up * act_slope).astype(BF16)
    up_grad = (act_grad * act_val).astype(BF16)
    grad_down = jnp.einsum("efr,erd->efd", activation, gated, preferred_element_type=F32).astype(BF16)
    grad_gate = jnp.einsum("efr,erd->efd", gate_grad, inputs, preferred_element_type=F32).astype(BF16)
    grad_up = jnp.einsum("efr,erd->efd", up_grad, inputs, preferred_element_type=F32).astype(BF16)
    hidden_part = jnp.einsum(
        "efr,efd->erd", gate_grad, w_gate, preferred_element_type=F32
    ) + jnp.einsum("efr,efd->erd", up_grad, w_up, preferred_element_type=F32)
    hidden_part = hidden_part.reshape(per_device, groups, shards, CAP, model_width)
    own_part = lax.psum_scatter(hidden_part, "grp", scatter_dimension=1, tiled=True)
    returned = lax.all_to_all(own_part, "shard", split_axis=2, concat_axis=2, tiled=True)
    moe_grad = jnp.einsum(
        "tesc,escd->td",
        token_map.reshape(tokens_here, per_device, shards, CAP),
        returned.reshape(per_device, shards, CAP, model_width),
        precision=lax.Precision.HIGHEST,
        preferred_element_type=F32,
    )
    input_grad = (out_grad.astype(F32) + moe_grad).astype(BF16)
    return (input_grad, grad_gate, grad_up, grad_down)


def solution(mesh):
    groups, shards = mesh.shape["grp"], mesh.shape["shard"]
    per_device = EXPERTS // shards
    tiles = per_device * CAP // TILE
    fits = (
        groups == 4
        and shards & (shards - 1) == 0
        and per_device * CAP == tiles * TILE
        and per_device == PER_TILE * tiles + 1
        and tiles == CAP
    )
    tokens = P(("grp", "shard"), None)
    weights = P("shard", "grp", None)
    return jax.shard_map(
        body if fits else plain_body,
        mesh=mesh,
        in_specs=(tokens, tokens, tokens, tokens, weights, weights, weights),
        out_specs=(tokens, weights, weights, weights),
        check_vma=False,
    )
```

time: 488 us -> 237 us (0.49)
  Pallas kernels: 0 us -> 218 us
  waiting for transfers between devices: 192 us -> 0 us
  matrix products: 116 us -> 5.04 us
  blocking collectives: 101 us -> 0 us
  local copies, waits for them, and re-layouts: 45.9 us -> 6 us
  between operations: 14.3 us -> 0.75 us
    pallas_call x0 -> x2, Pallas kernels: none -> 218 us  [the longest x1 201 us: exchange(): pl.pallas_call(functools.partial(exchange_kernel, order), out_shape=(jax....]
    unnamed x4 -> x0, waiting for transfers between devices: 121 us -> none
    dot_general x12 -> x3, matrix products: 116 us -> 5.04 us  [the longest x1 2.8 us: body(): moe_grad = jnp.dot(token_map, returned, preferred_element_type=F32)]
    all_to_all x3 -> x0, blocking collectives: 93 us -> none  [the longest x1 44.1 us: body(): lax.all_to_all(input_slots.reshape(slot_shape), 'shard', split_axis=1, co...]
    all_gather x2 -> x0, waiting for transfers between devices: 50.7 us -> none  [the longest x1 46.9 us: body(): lax.all_gather(arrived[1], 'grp', axis=1, tiled=True)]
    reshape x9 -> x0, local copies, waits for them, and re-layouts: 23.3 us -> none  [the longest x1 11.5 us: body(): hidden_part.reshape(per_device, groups, shards, CAP, model_width)]
    all_to_all x1 -> x0, waiting for transfers between devices: 20.4 us -> none  [body(): lax.all_to_all(own_part, 'shard', split_axis=2, concat_axis=2, tiled=True)]
    add x1 -> x0, local copies, waits for them, and re-layouts: 16.8 us -> none  [body(): jnp.einsum('efr,efd->erd', gate_grad, w_gate, preferred_element_type=jnp....]
  transfers between devices with their start and end apart: 4 -> 0, of which waited for: 4 -> 0; matrix products, arithmetic and copies ran while one was open for 18% -> 0% of each run, Pallas kernels for 0% -> 0%
where the time goes in v2:
time: 237 us; the launch traced here: 235 us
  Pallas kernels  218 us (92%)
  local copies, waits for them, and re-layouts  6 us (3%)
  matrix products  5.04 us (2%)
  other arithmetic  4.75 us (2%)
    pallas_call x1, Pallas kernels, exchange(): pl.pallas_call(functools.partial(exchange_kernel, order), out_shape=(jax....  201 us
    pallas_call x1, Pallas kernels, grads(): pl.pallas_call(grads_kernel, grid=(count,), out_shape=(grad, grad, grad),...  17 us
    unnamed x12, local copies, waits for them, and re-layouts  5.39 us

profile of v2, /device:TPU:0, one launch (start us, length us, event | category | flops | bytes accessed | tf_op | source)
XLA Modules:
  0.0 234.6 jit_solution(16191697288368772829)
XLA Ops:
  0.6 0.0 copy-start
  0.6 0.7 convert_element_type.33
  1.4 0.8 copy.37
  2.2 0.1 eq.60
  2.3 0.1 eq.56
  2.4 0.1 copy.39
  2.6 0.2 fusion.3
  2.9 0.2 fusion.5
  3.0 0.1 reduce_sum.21
  3.2 0.1 copy.41
  3.3 0.7 fusion.11
  4.0 0.1 fusion.1
  4.1 0.1 select_reduce_fusion
  4.2 0.7 fusion.2.perm_ref
  4.9 1.6 convolution_convert_fusion
  6.6 0.0 copy-done
  6.6 0.6 convolution_convert_fusion.1
  7.2 1.9 pad_maximum_fusion.rows_ref
  9.1 0.0 copy-start.4
  9.1 201.1 %exchange.1 = (bf16[2,16,96,2048]{3,2,1,0:T(8,128)(2,1)}, bf16[3,16,96,192]{3,2,1,0:T(8,128)(2,1)}, bf16[8,48,2048]{2,1,0:T(8,128)(2,1)}) custom-call(bf16[2,8,48,2048]{3,2,1,0:T(8,128)(2,1)} %pad_maximum_fusion.rows_ref, bf16[16,192,2048]{2,1,0:T(8,128)(2,1)} %wg_ref.1, bf16[16,192,2048]{2,1,0:T(8,128)(2,1)} %wu_ref.1, bf16[16,192,2048]{2,1,0:T(8,128)(2,1)} %wd_ref.1, ...), custom_call_target="tpu_custom_call" | custom-call | tf_op jit(solution)/shard_map/exchange/pallas_call | solution.py:309
  210.2 0.0 copy-start.3
  210.2 0.0 copy-done.4
  210.2 2.8 %fusion = bf16[128,2048]{1,0:T(8,128)(2,1)} fusion(pred[128,384]{1,0:T(8,128)(4,1)S(1)} %fusion.1, bf16[384,2048]{1,0:T(8,128)(2,1)} %bitcast.24, bf16[128,2048]{1,0:T(8,128)(2,1)S(1)} %copy-done.4), kind=kOutput, calls=%fused_computation.4 | convolution fusion | flops 202113024 | bytes 2670592 | tf_op jit(solution)/shard_map/dot_general | solution.py:397
  213.0 0.0 copy-done.3
  213.0 0.0 copy-start.2
  213.0 4.6 %copy-done.2 = bf16[2,16,96,2048]{3,2,1,0:T(8,128)(2,1)S(1)} copy-done((bf16[2,16,96,2048]{3,2,1,0:T(8,128)(2,1)S(1)}, bf16[2,16,96,2048]{3,2,1,0:T(8,128)(2,1)}, u32[]{:S(2)}) %copy-start.2) | copy-done | bytes 12582936
  217.6 0.0 copy-start.1
  217.6 17.0 %grads.1 = (bf16[16,192,2048]{2,1,0:T(8,128)(2,1)}, bf16[16,192,2048]{2,1,0:T(8,128)(2,1)}, bf16[16,192,2048]{2,1,0:T(8,128)(2,1)}) custom-call(bf16[2,16,96,2048]{3,2,1,0:T(8,128)(2,1)S(1)} %copy-done.2, bf16[3,16,96,192]{3,2,1,0:T(8,128)(2,1)S(1)} %copy-done.3), custom_call_target="tpu_custom_call" | custom-call | tf_op jit(solution)/shard_map/grads/pallas_call | solution.py:350
  234.6 0.0 copy-done.1
  (7 shorter events, 0.1 us)
Async XLA Ops:
  0.6 5.9 %copy-start = (bf16[128,2048]{1,0:T(8,128)(2,1)S(1)}, bf16[128,2048]{1,0:T(8,128)(2,1)}, u32[]{:S(2)}) copy-start(bf16[128,2048]{1,0:T(8,128)(2,1)} %param.7) | copy-start | bytes 1572868
  9.1 201.1 %copy-start.4 = (bf16[128,2048]{1,0:T(8,128)(2,1)S(1)}, bf16[128,2048]{1,0:T(8,128)(2,1)}, u32[]{:S(2)}) copy-start(bf16[128,2048]{1,0:T(8,128)(2,1)} %param.8) | copy-start | bytes 1572868
  210.2 2.8 %copy-start.3 = (bf16[3,16,96,192]{3,2,1,0:T(8,128)(2,1)S(1)}, bf16[3,16,96,192]{3,2,1,0:T(8,128)(2,1)}, u32[]{:S(2)}) copy-start(bf16[3,16,96,192]{3,2,1,0:T(8,128)(2,1)} %get-tuple-element.12.acts_ref) | copy-start | bytes 5308420
  213.0 4.6 %copy-start.2 = (bf16[2,16,96,2048]{3,2,1,0:T(8,128)(2,1)S(1)}, bf16[2,16,96,2048]{3,2,1,0:T(8,128)(2,1)}, u32[]{:S(2)}) copy-start(bf16[2,16,96,2048]{3,2,1,0:T(8,128)(2,1)} %get-tuple-element.11.rows_ref) | copy-start | bytes 37748740
  217.6 17.0 %copy-start.1 = (bf16[128,2048]{1,0:T(8,128)(2,1)S(1)}, bf16[128,2048]{1,0:T(8,128)(2,1)}, u32[]{:S(2)}) copy-start(bf16[128,2048]{1,0:T(8,128)(2,1)} %param.7) | copy-start | bytes 1572868

commit v3 on v2

v3 whole, which is shorter than its diff:
```python
import functools

import jax
import jax.numpy as jnp
from jax import lax
from jax.experimental import pallas as pl
from jax.experimental.pallas import tpu as pltpu
from jax.sharding import PartitionSpec as P

EXPERTS = 128
TOP = 2
CAP = 3
TILE = 16
PER_TILE = TILE // CAP
MESH = pl.DeviceIdType.MESH
F32 = jnp.float32
BF16 = jnp.bfloat16


def silu_parts(pre_act):
    sigmoid_val = jax.nn.sigmoid(pre_act)
    return (pre_act * sigmoid_val, sigmoid_val * (1.0 + pre_act * (1.0 - sigmoid_val)))


def flip(index, bits):
    bit = 1
    while bit <= bits:
        if bits & bit:
            index = index + bit * (1 - 2 * ((index // bit) % 2))
        bit *= 2
    return index


def places(shards):
    grp, me = lax.axis_index("grp"), lax.axis_index("shard")
    peers = [flip(me, k) for k in range(shards)]
    return grp, me, flip(grp, 1), flip(grp, 2), flip(grp, 3), peers


def greet(grp, me, grp_x, grp_y, peers):
    barrier = pltpu.get_barrier_semaphore()
    for peer in peers[1:]:
        pl.semaphore_signal(barrier, inc=1, device_id=(grp, peer), device_id_type=MESH)
    for other in (grp_x, grp_y):
        pl.semaphore_signal(barrier, inc=1, device_id=(other, me), device_id_type=MESH)
    pl.semaphore_wait(barrier, len(peers) + 1)


def remote(src, dst, send_sem, recv_sem, device):
    return pltpu.make_async_remote_copy(
        src_ref=src, dst_ref=dst, send_sem=send_sem, recv_sem=recv_sem,
        device_id=device, device_id_type=MESH,
    )


OWN, BY_X, BY_BOTH, BY_Y = range(4)


def exchange_kernel(order, x_ref, gated_ref, wg_ref, wu_ref, wd_ref, perm_ref, sorted_ref, acts_ref, out_ref,
                    arrived, rows, hidden, parts, weights, from_x, from_y, mid_x, mid_y, end_x, end_y, done,
                    zs, xs, ys, fxs, fys, cx, cy, cx2, cy2, cz, w_sem, own_sem, sorted_sem):
    shards = len(order)
    grp, me, grp_x, grp_y, _, by_flip = places(shards)
    peers = [by_flip[k] for k in order]
    sources = (x_ref, gated_ref)
    kinds, groups, _, depth, width = arrived.shape
    tiles = depth // TILE
    half = shards // 2
    block = groups * half * TILE
    share = groups * half * CAP
    spare = groups * half
    odd = PER_TILE * tiles
    chunk = min(512, width)
    low, high = pl.ds(0, width // 2), pl.ds(width // 2, width // 2)
    by_last = (((1,), (1,)), ((), ()))
    by_first = (((0,), (0,)), ((), ()))
    on_x, on_y = (grp_x, me), (grp_y, me)

    def tile_rows(t):
        return pl.ds(t * TILE, TILE)

    def slots(h):
        return pl.ds(h * half, half)

    def weight_copies(e, slot):
        return [
            pltpu.make_async_copy(ref.at[e], weights.at[j, slot], w_sem.at[j, slot])
            for j, ref in enumerate((wg_ref, wu_ref, wd_ref))
        ]

    def fetch(e, slot):
        for copy in weight_copies(e, slot):
            copy.start()

    def to_neighbours(t, i):
        at = tile_rows(t)
        if i == 0:
            pieces = [(ref.at[me, at], (kind,)) for kind, ref in enumerate(sources)]
        else:
            pieces = [(arrived.at[:, OWN, i, at], (slice(None),))]
        pair = []
        for rel, sems, device in ((BY_X, xs, on_x), (BY_Y, ys, on_y)):
            pair.append([
                remote(src, arrived.at[kind + (rel, i, at)], sems.at[0, t, i, j], sems.at[1, t, i, j], device)
                for j, (src, kind) in enumerate(pieces)
            ])
        for copy in pair[0] + pair[1]:
            copy.start()
        direct[t, i] = pair

    def forward(t, i):
        at = tile_rows(t)
        for copy in direct[t, i][0]:
            copy.wait_recv()
        first = remote(
            arrived.at[0, BY_X, i, at], arrived.at[0, BY_BOTH, i, at], fys.at[0, t, i], fys.at[1, t, i], on_y
        )
        first.start()
        for copy in direct[t, i][1]:
            copy.wait_recv()
        second = remote(
            arrived.at[1, BY_Y, i, at], arrived.at[1, BY_BOTH, i, at], fxs.at[0, t, i], fxs.at[1, t, i], on_x
        )
        second.start()
        passed[t, i] = (first, second)

    def relay(n):
        t, i = steps[n]
        if i > 0:
            for copy in over_z[t, i]:
                copy.wait_recv()
        to_neighbours(t, i)
        if n >= lag:
            forward(*steps[n - lag])

    def sort(t):
        for i in range(shards):
            for copy in passed[t, i]:
                copy.wait_recv()

        def columns(c, _):
            cols = pl.ds(pl.multiple_of(c * chunk, chunk), chunk)
            for kind in range(kinds):
                for side in range(2):
                    part = arrived[
                        kind, :, side * half:(side + 1) * half, t * TILE:(t + 1) * TILE, cols
                    ].reshape(block, chunk)
                    placed = jnp.dot(perm_ref[...], part, preferred_element_type=F32).astype(BF16)
                    for j in range(PER_TILE):
                        rows[kind, t * PER_TILE + j, side * share:(side + 1) * share, cols] = (
                            placed[j * share:(j + 1) * share]
                        )
                    base = (2 * t + side) * spare
                    rows[kind, odd, base:base + spare, cols] = placed[PER_TILE * share:]
            return 0

        lax.fori_loop(0, width // chunk, columns, 0)
        spans = [pl.ds(t * PER_TILE, PER_TILE)] + ([pl.ds(odd, 1)] if t == tiles - 1 else [])
        for j, span in enumerate(spans):
            copy = pltpu.make_async_copy(rows.at[:, span], sorted_ref.at[:, span], sorted_sem.at[t + j])
            copy.start()
            written.append(copy)

    def products(e, slot, span, j):
        for copy in weight_copies(e, slot):
            copy.wait()
        x = rows[0, e, span]
        gated = rows[1, e, span]
        wg, wu = weights[0, slot], weights[1, slot]
        pre_gate = lax.dot_general(x, wg, by_last, preferred_element_type=F32)
        pre_up = lax.dot_general(x, wu, by_last, preferred_element_type=F32)
        act_grad = lax.dot_general(gated, weights[2, slot], by_last, preferred_element_type=F32)
        act_val, act_slope = silu_parts(pre_gate)
        gate_grad = (act_grad * pre_up * act_slope).astype(BF16)
        up_grad = (act_grad * act_val).astype(BF16)
        acts_ref[0, e, span] = (act_val * pre_up).astype(BF16)
        acts_ref[1, e, span] = gate_grad
        acts_ref[2, e, span] = up_grad
        hidden[j, pl.ds(0, span.size)] = (
            jnp.dot(gate_grad, wg, preferred_element_type=F32)
            + jnp.dot(up_grad, wu, preferred_element_type=F32)
        ).astype(BF16)

    def whole_experts(t, begin, end):
        def one(j, _):
            e = t * PER_TILE + j
            fetch(e + 1 + (j + 1) // PER_TILE * (odd - (t + 1) * PER_TILE), (j + 1) % 2)
            products(e, j % 2, pl.ds(0, 2 * share), j)
            return 0

        lax.fori_loop(begin, end, one, 0)

    def odd_expert(t):
        slot = PER_TILE % 2
        if t + 1 < tiles:
            fetch((t + 1) * PER_TILE, 1 - slot)
        products(odd, slot, pl.ds(2 * t * spare, 2 * spare), PER_TILE)

    def unsort(t):
        def columns(c, _):
            cols = pl.ds(pl.multiple_of(c * chunk, chunk), chunk)
            for side in range(2):
                spans = [hidden[j, side * share:(side + 1) * share, cols] for j in range(PER_TILE)]
                spans.append(hidden[PER_TILE, side * spare:(side + 1) * spare, cols])
                back = lax.dot_general(
                    perm_ref[...], jnp.concatenate(spans, axis=0), by_first, preferred_element_type=F32
                ).astype(BF16)
                parts[
                    :, side * half:(side + 1) * half, t * TILE:(t + 1) * TILE, cols
                ] = back.reshape(groups, half, TILE, chunk)
            return 0

        lax.fori_loop(0, width // chunk, columns, 0)

    def first(t, h):
        at = tile_rows(t)
        to_x = remote(
            parts.at[pl.ds(BY_X, 2), slots(h), at, low], from_x.at[t, h], cx.at[0, t, h], cx.at[1, t, h], on_x
        )
        to_y = remote(
            parts.at[pl.ds(BY_BOTH, 2), slots(h), at, high], from_y.at[t, h], cy.at[0, t, h], cy.at[1, t, h], on_y
        )
        to_x.start()
        to_y.start()
        starts[t, h] = (to_x, to_y)

    def second(t, h):
        at = tile_rows(t)
        starts[t, h][0].wait_recv()
        mid_x[t, h] = (parts[BY_Y, slots(h), at, low].astype(F32) + from_x[t, h, 1].astype(F32)).astype(BF16)
        to_y = remote(mid_x.at[t, h], end_y.at[t, h], cy2.at[0, t, h], cy2.at[1, t, h], on_y)
        to_y.start()
        starts[t, h][1].wait_recv()
        mid_y[t, h] = (parts[BY_X, slots(h), at, high].astype(F32) + from_y[t, h, 0].astype(F32)).astype(BF16)
        to_x = remote(mid_y.at[t, h], end_x.at[t, h], cx2.at[0, t, h], cx2.at[1, t, h], on_x)
        to_x.start()
        middles[t, h] = (to_y, to_x)

    def third(t, h):
        at = tile_rows(t)
        middles[t, h][0].wait_recv()
        done[t, h, :, :, low] = (
            parts[OWN, slots(h), at, low].astype(F32) + from_x[t, h, 0].astype(F32) + end_y[t, h].astype(F32)
        ).astype(BF16)
        middles[t, h][1].wait_recv()
        done[t, h, :, :, high] = (
            parts[OWN, slots(h), at, high].astype(F32) + from_y[t, h, 1].astype(F32) + end_x[t, h].astype(F32)
        ).astype(BF16)
        for j in range(half - 1, -1, -1):
            i = h * half + j
            if i == 0:
                out_ref[me, at] = done[t, h, 0]
            else:
                copy = remote(
                    done.at[t, h, j], out_ref.at[me, at], cz.at[0, t, i], cz.at[1, t, i], (grp, peers[i])
                )
                copy.start()
                returns.append(copy)

    direct, over_z, passed, starts, middles = {}, {}, {}, {}, {}
    returns, written = [], []
    steps = [(t, i) for t in range(tiles) for i in range(shards)]
    lag = 3
    fetch(0, 0)
    greet(grp, me, grp_x, grp_y, by_flip)
    relay(0)
    for t, i in steps:
        if i > 0:
            over_z[t, i] = [
                remote(
                    ref.at[peers[i], tile_rows(t)], arrived.at[kind, OWN, i, tile_rows(t)],
                    zs.at[0, t, i, kind], zs.at[1, t, i, kind], (grp, peers[i]),
                )
                for kind, ref in enumerate(sources)
            ]
            for copy in over_z[t, i]:
                copy.start()
    own = [
        pltpu.make_async_copy(ref.at[me], arrived.at[kind, OWN, 0], own_sem.at[kind])
        for kind, ref in enumerate(sources)
    ]
    for copy in own:
        copy.start()

    def work(t):
        tasks = [functools.partial(sort, t)]
        tasks += [functools.partial(whole_experts, t, j, j + 1) for j in range(PER_TILE)]
        return tasks + [functools.partial(odd_expert, t), functools.partial(unsort, t)]

    queue = []
    for n in range(1, len(steps)):
        relay(n)
        t, i = steps[n]
        if t == 0:
            continue
        if i == lag + 1:
            if t == 1:
                for copy in own:
                    copy.wait()
            queue += work(t - 1)
        for task in queue[:2]:
            task()
        queue = queue[2:]
        if t == 2 and i == 2:
            first(0, 0)
        if t == 2 and i == lag + 2:
            first(0, 1)
    for task in queue:
        task()
    for n in range(len(steps) - lag, len(steps)):
        forward(*steps[n])
    for t in range(1, tiles - 1):
        first(t, 0)
        first(t, 1)
    second(0, 0)
    tasks = work(tiles - 1)
    tasks[0]()
    units = [(t, h) for t in range(tiles - 1) for h in range(2)]
    for j, task in enumerate(tasks[1:]):
        task()
        if j + 1 < len(units):
            second(*units[j + 1])
        if j < len(units):
            third(*units[j])
    first(tiles - 1, 0)
    first(tiles - 1, 1)
    second(tiles - 1, 0)
    second(tiles - 1, 1)
    third(tiles - 1, 0)
    third(tiles - 1, 1)
    for step in steps:
        if step[1] > 0:
            for copy in over_z[step]:
                copy.wait_send()
        for copy in direct[step][0] + direct[step][1] + list(passed[step]):
            copy.wait_send()
    for unit in starts:
        for copy in starts[unit] + middles[unit]:
            copy.wait_send()
    for copy in written:
        copy.wait()
    for copy in returns:
        copy.wait()


def sort_matrix(sources):
    taken = jnp.arange(sources * TILE, dtype=jnp.int32)
    source, place = taken // TILE, taken % TILE
    goes = jnp.where(
        place < PER_TILE * CAP,
        place // CAP * (sources * CAP) + source * CAP + place % CAP,
        PER_TILE * CAP * sources + source,
    )
    return (goes[None, :] == taken[:, None]).astype(BF16)


def exchange(sent, gated, w_gate, w_up, w_down, groups):
    shards, depth, width = sent.shape
    count, units, _ = w_gate.shape
    row_count = groups * shards * CAP
    tiles = depth // TILE
    order = sorted(range(shards), key=lambda k: (k // 2 % 2, k))
    perm = sort_matrix(groups * shards // 2)
    half = pltpu.VMEM((tiles, 2, shards // 2, TILE, width // 2), BF16)
    pair = pltpu.VMEM((tiles, 2, 2, shards // 2, TILE, width // 2), BF16)
    sem = pltpu.SemaphoreType.DMA((2, tiles, shards))
    sem_kinds = pltpu.SemaphoreType.DMA((2, tiles, shards, 2))
    sem_halves = pltpu.SemaphoreType.DMA((2, tiles, 2))
    anywhere = pl.BlockSpec(memory_space=pl.ANY)
    near = pl.BlockSpec(memory_space=pltpu.VMEM)
    return pl.pallas_call(
        functools.partial(exchange_kernel, order),
        out_shape=(
            jax.ShapeDtypeStruct((2, count, row_count, width), BF16),
            jax.ShapeDtypeStruct((3, count, row_count, units), BF16),
            jax.ShapeDtypeStruct((shards, depth, width), BF16),
        ),
        in_specs=[anywhere] * 5 + [near],
        out_specs=(anywhere, near, near),
        scratch_shapes=[
            pltpu.VMEM((2, groups, shards, depth, width), BF16),
            pltpu.VMEM((2, count, row_count, width), BF16),
            pltpu.VMEM((PER_TILE + 1, row_count, width), BF16),
            pltpu.VMEM((groups, shards, depth, width), BF16),
            pltpu.VMEM((3, 2, units, width), BF16),
            pair, pair, half, half, half, half,
            pltpu.VMEM((tiles, 2, shards // 2, TILE, width), BF16),
            sem_kinds, sem_kinds, sem_kinds, sem, sem,
            sem_halves, sem_halves, sem_halves, sem_halves, sem,
            pltpu.SemaphoreType.DMA((3, 2)),
            pltpu.SemaphoreType.DMA((2,)),
            pltpu.SemaphoreType.DMA((tiles + 1,)),
        ],
        compiler_params=pltpu.CompilerParams(
            collective_id=0, has_side_effects=True, vmem_limit_bytes=60 * 1024 * 1024
        ),
        name="exchange",
    )(sent, gated, w_gate, w_up, w_down, perm)


def grads_kernel(rows_ref, acts_ref, gg_ref, gu_ref, gd_ref):
    by_first = (((0,), (0,)), ((), ()))
    x, gated = rows_ref[0, 0], rows_ref[1, 0]
    for ref, j, side in ((gd_ref, 0, gated), (gg_ref, 1, x), (gu_ref, 2, x)):
        ref[0] = lax.dot_general(acts_ref[j, 0], side, by_first, preferred_element_type=F32).astype(BF16)


def grads(rows, acts):
    kinds, count, row_count, width = rows.shape
    units = acts.shape[-1]
    grad = jax.ShapeDtypeStruct((count, units, width), BF16)
    out = pl.BlockSpec((1, units, width), lambda e: (e, 0, 0))
    return pl.pallas_call(
        grads_kernel,
        grid=(count,),
        out_shape=(grad, grad, grad),
        in_specs=[
            pl.BlockSpec((kinds, 1, row_count, width), lambda e: (0, e, 0, 0)),
            pl.BlockSpec((3, 1, row_count, units), lambda e: (0, e, 0, 0)),
        ],
        out_specs=(out, out, out),
        compiler_params=pltpu.CompilerParams(vmem_limit_bytes=60 * 1024 * 1024),
        name="grads",
    )(rows, acts)


def body(moe_input, out_grad, expert_ids, gate_weights, w_gate, w_up, w_down):
    contract_rows = (((0,), (0,)), ((), ()))
    shards = lax.axis_size("shard")
    groups = lax.axis_size("grp")
    per_device = w_gate.shape[0]
    tokens_here, model_width = moe_input.shape
    depth = per_device * CAP
    tiles = depth // TILE
    flat_ids = expert_ids.reshape(tokens_here * TOP)
    matches = (flat_ids[:, None] == jnp.arange(EXPERTS, dtype=jnp.int32)[None, :]).astype(jnp.int32)
    rank_of = jnp.sum((jnp.cumsum(matches, axis=0) - matches) * matches, axis=1)
    local = flat_ids % per_device
    odd = PER_TILE * tiles
    place = jnp.where(
        local < odd,
        local // PER_TILE * TILE + local % PER_TILE * CAP + rank_of,
        rank_of * TILE + PER_TILE * CAP,
    )
    slot_of = (flat_ids // per_device * depth + place).reshape(tokens_here, TOP)
    slots = jnp.arange(EXPERTS * CAP, dtype=jnp.int32)
    chosen = slot_of[:, :, None] == slots[None, None, :]
    token_map = jnp.any(chosen, axis=1).astype(BF16)
    gate_map = jnp.sum(
        jnp.where(chosen, gate_weights.astype(F32)[:, :, None], 0.0), axis=1
    ).astype(BF16)
    input_slots = lax.dot_general(token_map, moe_input, contract_rows, preferred_element_type=F32)
    gated_slots = lax.dot_general(gate_map, out_grad, contract_rows, preferred_element_type=F32)
    block = (shards, depth, model_width)
    sorted_rows, acts, returned = exchange(
        input_slots.astype(BF16).reshape(block), gated_slots.astype(BF16).reshape(block),
        w_gate, w_up, w_down, groups,
    )
    grad_gate, grad_up, grad_down = grads(sorted_rows, acts)
    returned = returned.reshape(shards * depth, model_width)
    moe_grad = jnp.dot(token_map, returned, preferred_element_type=F32)
    input_grad = (out_grad.astype(F32) + moe_grad).astype(BF16)
    return (input_grad, grad_gate, grad_up, grad_down)


def plain_slot_maps(ids_here, per_device, shards):
    tokens_here = ids_here.shape[0]
    flat_ids = ids_here.reshape(tokens_here * TOP)
    matches = (flat_ids[:, None] == jnp.arange(EXPERTS, dtype=jnp.int32)[None, :]).astype(jnp.int32)
    rank_of = jnp.sum((jnp.cumsum(matches, axis=0) - matches) * matches, axis=1)
    slot_of = flat_ids % per_device * (shards * CAP) + flat_ids // per_device * CAP + rank_of
    return (slot_of[:, None] == jnp.arange(EXPERTS * CAP, dtype=jnp.int32)[None, :]).astype(F32)


def plain_body(moe_input, out_grad, expert_ids, gate_weights, w_gate, w_up, w_down):
    contract_rows = (((0,), (0,)), ((), ()))
    shards = lax.axis_size("shard")
    groups = lax.axis_size("grp")
    per_device = w_gate.shape[0]
    tokens_here, model_width = moe_input.shape
    slot_total = EXPERTS * CAP
    chosen = plain_slot_maps(expert_ids, per_device, shards).reshape(tokens_here, TOP, slot_total)
    token_map = jnp.sum(chosen, axis=1)
    gate_map = jnp.sum(chosen * gate_weights.astype(F32)[:, :, None], axis=1).astype(BF16)
    slot_shape = (per_device, shards, CAP, model_width)
    row_count = groups * shards * CAP

    def send(mapping, rows):
        slots = lax.dot_general(mapping, rows, contract_rows, preferred_element_type=F32).astype(BF16)
        arrived = lax.all_to_all(
            slots.reshape(slot_shape), "shard", split_axis=1, concat_axis=1, tiled=True
        )
        gathered = lax.all_gather(arrived, "grp", axis=1, tiled=True)
        return gathered.reshape(per_device, row_count, model_width)

    inputs = send(token_map.astype(BF16), moe_input)
    gated = send(gate_map, out_grad)
    pre_gate = jnp.einsum("efd,erd->efr", w_gate, inputs, preferred_element_type=F32)
    pre_up = jnp.einsum("efd,erd->efr", w_up, inputs, preferred_element_type=F32)
    act_val, act_slope = silu_parts(pre_gate)
    activation = (act_val * pre_up).astype(BF16)
    act_grad = jnp.einsum("efd,erd->efr", w_down, gated, preferred_element_type=F32)
    gate_grad = (act_grad * pre_up * act_slope).astype(BF16)
    up_grad = (act_grad * act_val).astype(BF16)
    grad_down = jnp.einsum("efr,erd->efd", activation, gated, preferred_element_type=F32).astype(BF16)
    grad_gate = jnp.einsum("efr,erd->efd", gate_grad, inputs, preferred_element_type=F32).astype(BF16)
    grad_up = jnp.einsum("efr,erd->efd", up_grad, inputs, preferred_element_type=F32).astype(BF16)
    hidden_part = jnp.einsum(
        "efr,efd->erd", gate_grad, w_gate, preferred_element_type=F32
    ) + jnp.einsum("efr,efd->erd", up_grad, w_up, preferred_element_type=F32)
    hidden_part = hidden_part.reshape(per_device, groups, shards, CAP, model_width)
    own_part = lax.psum_scatter(hidden_part, "grp", scatter_dimension=1, tiled=True)
    returned = lax.all_to_all(own_part, "shard", split_axis=2, concat_axis=2, tiled=True)
    moe_grad = jnp.einsum(
        "tesc,escd->td",
        token_map.reshape(tokens_here, per_device, shards, CAP),
        returned.reshape(per_device, shards, CAP, model_width),
        precision=lax.Precision.HIGHEST,
        preferred_element_type=F32,
    )
    input_grad = (out_grad.astype(F32) + moe_grad).astype(BF16)
    return (input_grad, grad_gate, grad_up, grad_down)


def solution(mesh):
    groups, shards = mesh.shape["grp"], mesh.shape["shard"]
    per_device = EXPERTS // shards
    tiles = per_device * CAP // TILE
    fits = (
        groups == 4
        and shards & (shards - 1) == 0
        and per_device * CAP == tiles * TILE
        and per_device == PER_TILE * tiles + 1
        and tiles == CAP
    )
    tokens = P(("grp", "shard"), None)
    weights = P("shard", "grp", None)
    return jax.shard_map(
        body if fits else plain_body,
        mesh=mesh,
        in_specs=(tokens, tokens, tokens, tokens, weights, weights, weights),
        out_specs=(tokens, weights, weights, weights),
        check_vma=False,
    )
```

time: 237 us -> 223 us (0.941)
  Pallas kernels: 218 us -> 210 us
  local copies, waits for them, and re-layouts: 6 us -> 1.42 us
    pallas_call x1, Pallas kernels: 201 us -> 187 us  [exchange(): pl.pallas_call(functools.partial(exchange_kernel, order), out_shape=(jax....]
    pallas_call x1, Pallas kernels: 17 us -> 23.2 us  [grads(): pl.pallas_call(grads_kernel, grid=(count,), out_shape=(grad, grad, grad),...]
    unnamed x12 -> x8, local copies, waits for them, and re-layouts: 5.39 us -> 0.81 us
where the time goes in v3:
time: 223 us; the launch traced here: 222 us
  Pallas kernels  210 us (94%)
  matrix products  7.18 us (3%)
  other arithmetic  2.82 us (1%)
    pallas_call x1, Pallas kernels, exchange(): pl.pallas_call(functools.partial(exchange_kernel, order), out_shape=(jax....  187 us
    pallas_call x1, Pallas kernels, grads(): pl.pallas_call(grads_kernel, grid=(count,), out_shape=(grad, grad, grad),...  23.2 us

profile of v3, /device:TPU:0, one launch (start us, length us, event | category | flops | bytes accessed | tf_op | source)
XLA Modules:
  0.0 222.5 jit_solution(11782476076212770179)
XLA Ops:
  0.6 0.0 copy-start
  0.6 0.7 convert_element_type.33
  1.4 0.8 copy.37
  2.2 0.1 eq.60
  2.3 0.1 eq.56
  2.4 0.1 copy.39
  2.6 0.2 fusion.3
  2.9 0.2 fusion.5
  3.0 0.1 reduce_sum.21
  3.2 0.1 copy.41
  3.3 0.7 fusion.11
  4.0 0.1 fusion.1
  4.1 0.1 select_reduce_fusion
  4.2 0.7 fusion.2.perm_ref
  4.9 2.8 %convolution_convert_fusion = bf16[384,2048]{1,0:T(8,128)(2,1)} fusion(bf16[128,2048]{1,0:T(8,128)(2,1)} %param.8, bf16[128,384]{1,0:T(8,128)(2,1)S(1)} %select_reduce_fusion), kind=kOutput, calls=%fused_computation | convolution fusion | flops 202113024 | bytes 2195456 | tf_op jit(solution)/shard_map/dot_general | solution.py:453
  7.7 0.0 copy-done
  7.7 1.8 convolution_convert_fusion.1
  9.5 0.0 copy-start.2
  9.5 187.2 %exchange.1 = (bf16[2,16,96,2048]{3,2,1,0:T(8,128)(2,1)}, bf16[3,16,96,192]{3,2,1,0:T(8,128)(2,1)}, bf16[8,48,2048]{2,1,0:T(8,128)(2,1)}) custom-call(bf16[8,48,2048]{2,1,0:T(8,128)(2,1)} %bitcast.23, bf16[8,48,2048]{2,1,0:T(8,128)(2,1)} %bitcast.22, bf16[16,192,2048]{2,1,0:T(8,128)(2,1)} %wg_ref.1, bf16[16,192,2048]{2,1,0:T(8,128)(2,1)} %wu_ref.1, ...), custom_call_target="tpu_custom_call" | custom-call | tf_op jit(solution)/shard_map/exchange/pallas_call | solution.py:371
  196.6 0.0 copy-done.2
  196.6 2.6 %fusion = bf16[128,2048]{1,0:T(8,128)(2,1)} fusion(pred[128,384]{1,0:T(8,128)(4,1)S(1)} %fusion.1, bf16[384,2048]{1,0:T(8,128)(2,1)} %bitcast.24, bf16[128,2048]{1,0:T(8,128)(2,1)S(1)} %copy-done.2), kind=kOutput, calls=%fused_computation.3 | convolution fusion | flops 202113024 | bytes 2670592 | tf_op jit(solution)/shard_map/dot_general | solution.py:461
  199.3 0.0 copy-start.1
  199.3 23.2 %grads.1 = (bf16[16,192,2048]{2,1,0:T(8,128)(2,1)}, bf16[16,192,2048]{2,1,0:T(8,128)(2,1)}, bf16[16,192,2048]{2,1,0:T(8,128)(2,1)}) custom-call(bf16[2,16,96,2048]{3,2,1,0:T(8,128)(2,1)} %get-tuple-element.11.rows_ref, bf16[3,16,96,192]{3,2,1,0:T(8,128)(2,1)} %get-tuple-element.12.acts_ref), custom_call_target="tpu_custom_call" | custom-call | tf_op jit(solution)/shard_map/grads/pallas_call | solution.py:413
  222.5 0.0 copy-done.1
  (7 shorter events, 0.1 us)
Async XLA Ops:
  0.6 7.1 %copy-start = (bf16[128,2048]{1,0:T(8,128)(2,1)S(1)}, bf16[128,2048]{1,0:T(8,128)(2,1)}, u32[]{:S(2)}) copy-start(bf16[128,2048]{1,0:T(8,128)(2,1)} %param.7) | copy-start | bytes 1572868
  9.5 187.2 %copy-start.2 = (bf16[128,2048]{1,0:T(8,128)(2,1)S(1)}, bf16[128,2048]{1,0:T(8,128)(2,1)}, u32[]{:S(2)}) copy-start(bf16[128,2048]{1,0:T(8,128)(2,1)} %param.8) | copy-start | bytes 1572868
  199.3 23.2 %copy-start.1 = (bf16[128,2048]{1,0:T(8,128)(2,1)S(1)}, bf16[128,2048]{1,0:T(8,128)(2,1)}, u32[]{:S(2)}) copy-start(bf16[128,2048]{1,0:T(8,128)(2,1)} %param.7) | copy-start | bytes 1572868
